TPU v7x, 32 devices: a whole 2x2x4 slice. The times are simulated.
32 devices in a mesh: seq: 32 (over z, y, x, core), wt: 1.
Axes of the slice: x: 2, y: 2, z: 4, core: 2. Of those that a mesh axis runs over, the one named last changes fastest.
Arguments:
- hidden_rows: bfloat16 [8192, 2688], P('seq'), may hold values from -6 to 6
- value_weight: bfloat16 [2688, 1536], P('seq', 'wt'), may hold values from -0.125 to 0.125
- queries: bfloat16 [8192, 3072], P('seq', 'wt'), may hold values from -60 to 60
- key_rows: bfloat16 [8192, 1536], P('seq', 'wt'), may hold values from -4.1 to 4.1
- out_grad: bfloat16 [8192, 3072], P('seq', 'wt'), may hold values from -6 to 6
- segments: int32 [8192], replicated, may hold values from 0 to 3, never falling along the last dimension, each value on 1 to 4096 neighbouring positions
Outputs:
- attention: bfloat16 [8192, 3072], P('seq', 'wt')
- weight_grad: float32 [2688, 1536], P('seq', 'wt')
Inputs may be any that keep to these rules, and one draw needn't show every extreme that they name: `segments`: never falling along the slab.
All inputs are finite; a program needn't handle non-finite values.
Results may differ from a plain program's by a relative error of at most 0.0057.
Values may be sent and summed in bfloat16 or wider, within the bound.
A program may use at most 128 MiB of HBM per device.

v0:
```python
import math

import jax
import jax.numpy as jnp
from jax import lax
from jax.sharding import PartitionSpec as P

HD = 128
WINDOW = 1024


def passed_along(block, axis, distance):
    devices = range(lax.axis_size(axis))
    route = [(i - distance, i) for i in devices if i - distance in devices]
    return lax.ppermute(block, axis, route)


def attend(query_four, grad_four, key_three, value_three, allowed, scale):
    scores = (
        jnp.einsum("tkgd,lkd->kgtl", query_four, key_three, preferred_element_type=jnp.float32)
        * scale
    )
    scores = jnp.where(allowed[None, None], scores, -1e30)
    highest = jnp.max(scores, axis=-1, keepdims=True)
    weights = jnp.exp(scores - highest)
    probs = (weights / jnp.sum(weights, axis=-1, keepdims=True)).astype(jnp.bfloat16)
    output = jnp.einsum("kgtl,lkd->tkgd", probs, value_three, preferred_element_type=jnp.float32)
    partial_value = jnp.einsum(
        "kgtl,tkgd->lkd", probs, grad_four, preferred_element_type=jnp.float32
    )
    return (output, partial_value)


def per_device(hidden_rows, value_weight, queries, key_rows, out_grad, segments):
    rows_here = hidden_rows.shape[0]
    kv_width = value_weight.shape[1]
    kv_heads = kv_width // HD
    group_size = queries.shape[1] // kv_width
    blocks_back = (WINDOW + rows_here - 2) // rows_here
    key_span = (blocks_back + 1) * rows_here
    padding = blocks_back * rows_here
    scale = 1.0 / math.sqrt(HD)
    columns = hidden_rows
    values = jnp.dot(
        columns,
        lax.all_gather(value_weight, "seq", axis=0, tiled=True),
        preferred_element_type=jnp.float32,
    ).astype(jnp.bfloat16)
    earlier = [passed_along((key_rows, values), "seq", offset + 1) for offset in range(blocks_back)]
    ordered = list(reversed(earlier))
    key_window = jnp.concatenate([member[0] for member in ordered] + [key_rows], axis=0)
    value_window = jnp.concatenate([member[1] for member in ordered] + [values], axis=0)
    position = lax.axis_index("seq")
    segs_padded = jnp.concatenate([jnp.full((padding,), -1, jnp.int32), segments], axis=0)
    key_seg = lax.dynamic_slice_in_dim(segs_padded, position * rows_here, key_span, 0)
    query_seg = lax.dynamic_slice_in_dim(segments, position * rows_here, rows_here, 0)
    distance = (
        jnp.arange(rows_here, dtype=jnp.int32)[:, None]
        + padding
        - jnp.arange(key_span, dtype=jnp.int32)[None, :]
    )
    allowed = (distance >= 0) & (distance < WINDOW) & (query_seg[:, None] == key_seg[None, :])
    query_four = queries.reshape(rows_here, kv_heads, group_size, HD)
    grad_four = out_grad.reshape(rows_here, kv_heads, group_size, HD)
    key_three = key_window.reshape(key_span, kv_heads, HD)
    value_three = value_window.reshape(key_span, kv_heads, HD)
    output, partial_value = attend(query_four, grad_four, key_three, value_three, allowed, scale)
    attention = output.reshape(rows_here, kv_width * group_size).astype(jnp.bfloat16)
    partial_value = partial_value.reshape(key_span, kv_width).astype(jnp.bfloat16)
    gathered = partial_value[padding:].astype(jnp.float32)
    for offset in range(1, blocks_back + 1):
        portion = partial_value[
            (blocks_back - offset) * rows_here : (blocks_back - offset + 1) * rows_here
        ]
        gathered = gathered + passed_along(portion, "seq", -offset).astype(jnp.float32)
    value_grad = gathered.astype(jnp.bfloat16)
    columns = hidden_rows
    weight_grad = lax.psum_scatter(
        lax.dot_general(
            columns, value_grad, (((0,), (0,)), ((), ())), preferred_element_type=jnp.float32
        ),
        "seq",
        scatter_dimension=0,
        tiled=True,
    )
    return (attention, weight_grad)


def solution(mesh):
    in_specs = (P("seq", None), P("seq", "wt"), P("seq", "wt"), P("seq", "wt"), P("seq", "wt"), P())
    out_specs = (P("seq", "wt"), P("seq", "wt"))
    return jax.shard_map(
        per_device, mesh=mesh, in_specs=in_specs, out_specs=out_specs, check_vma=False
    )
```

profile of v0, /device:TPU:16, one launch (start us, length us, event | category | flops | bytes accessed | tf_op | source)
XLA Modules:
  0.0 569.4 jit_solution(9073879779665016051)
XLA Ops:
  9.4 3.4 collective-permute-start.4
  12.8 2.6 collective-permute-start.5
  15.4 3.4 collective-permute-start.6
  18.8 2.6 collective-permute-start.7
  23.4 5.0 reshape.86
  28.4 2.6 copy.48
  31.1 35.3 %collective-permute-done.4 = bf16[256,1536]{0,1:T(8,128)(2,1)} collective-permute-done((bf16[256,1536]{0,1:T(8,128)(2,1)S(1)}, bf16[256,1536]{0,1:T(8,128)(2,1)}, u32[]{:S(2)}, u32[]{:S(2)}) %collective-permute-start.4) | collective-permute-done | bytes 786464 | tf_op jit(solution)/shard_map/ppermute | solution.py:15
  68.8 7.1 %collective-permute-done.6 = bf16[256,1536]{0,1:T(8,128)(2,1)} collective-permute-done((bf16[256,1536]{0,1:T(8,128)(2,1)S(1)}, bf16[256,1536]{0,1:T(8,128)(2,1)}, u32[]{:S(2)}, u32[]{:S(2)}) %collective-permute-start.6) | collective-permute-done | bytes 786464 | tf_op jit(solution)/shard_map/ppermute | solution.py:15
  77.1 14.8 %collective-permute-done.7 = bf16[256,1536]{0,1:T(8,128)(2,1)S(1)} collective-permute-done((bf16[256,1536]{0,1:T(8,128)(2,1)S(1)}, bf16[256,1536]{0,1:T(8,128)(2,1)S(1)}, u32[]{:S(2)}, u32[]{:S(2)}) %collective-permute-start.7) | collective-permute-done | bytes 786464 | tf_op jit(solution)/shard_map/ppermute | solution.py:15
  93.9 18.3 %fusion.27 = (f32[12,2,256]{2,1,0:T(2,128)S(1)}, f32[12,2,256,1280]{2,3,1,0:T(8,128)}) fusion(pred[256,1280]{0,1:T(8,128)(4,1)S(1)} %fusion.22, bf16[1280,12,128,1]{0,2,3,1:T(8,128)(2,1)} %bitcast.61, bf16[256,12,2,128]{3,2,1,0:T(2,128)(2,1)} %reshape.86), kind=kOutput, calls=%fused_computation.43 | convolution fusion | flops 2044724480 | bytes 37314560 | tf_op jit(solution)/shard_map/sub | solution.py:25
  112.2 17.1 %divide_convert_fusion = bf16[12,2,256,1280]{2,3,1,0:T(8,128)(2,1)} fusion(f32[12,2,256,1280]{2,3,1,0:T(8,128)} %get-tuple-element.14, f32[12,2,256]{2,1,0:T(2,128)S(1)} %get-tuple-element.13), kind=kLoop, calls=%fused_computation.2 | loop fusion | flops 15728640 | bytes 47210496 | tf_op jit(solution)/shard_map/convert_element_type | solution.py:26
  129.3 8.6 %fusion.5 = bf16[1280,12,128]{0,2,1:T(8,128)(2,1)S(1)} fusion(bf16[12,2,256,1280]{2,3,1,0:T(8,128)(2,1)} %divide_convert_fusion, bf16[256,12,2,128]{0,3,2,1:T(8,128)(2,1)S(1)} %bitcast.55), kind=kOutput, calls=%fused_computation.10 | convolution fusion | flops 2015232000 | bytes 21233664 | tf_op jit(solution)/shard_map/kgtl,tkgd->lkd/dot_general | solution.py:28
  142.2 4.9 collective-permute-start.8
  149.0 9.2 %collective-permute-done.10 = bf16[256,1536]{0,1:T(8,128)(2,1)S(1)} collective-permute-done((bf16[256,1536]{0,1:T(8,128)(2,1)S(1)}, bf16[256,1536]{0,1:T(8,128)(2,1)S(1)}, u32[]{:S(2)}, u32[]{:S(2)}) %collective-permute-start.10) | collective-permute-done | bytes 786464 | tf_op jit(solution)/shard_map/ppermute | solution.py:15
  158.2 12.7 %collective-permute-done.11 = bf16[256,1536]{0,1:T(8,128)(2,1)S(1)} collective-permute-done((bf16[256,1536]{0,1:T(8,128)(2,1)S(1)}, bf16[256,1536]{0,1:T(8,128)(2,1)S(1)}, u32[]{:S(2)}, u32[]{:S(2)}) %collective-permute-start.11) | collective-permute-done | bytes 786464 | tf_op jit(solution)/shard_map/ppermute | solution.py:15
  170.9 10.4 %collective-permute-done.8 = bf16[256,1536]{0,1:T(8,128)(2,1)S(1)} collective-permute-done((bf16[256,1536]{0,1:T(8,128)(2,1)S(1)}, bf16[256,1536]{0,1:T(8,128)(2,1)S(1)}, u32[]{:S(2)}, u32[]{:S(2)}) %collective-permute-start.8) | collective-permute-done | bytes 786464 | tf_op jit(solution)/shard_map/ppermute | solution.py:15
  181.3 8.4 %collective-permute-done.9 = bf16[256,1536]{0,1:T(8,128)(2,1)S(1)} collective-permute-done((bf16[256,1536]{0,1:T(8,128)(2,1)S(1)}, bf16[256,1536]{0,1:T(8,128)(2,1)S(1)}, u32[]{:S(2)}, u32[]{:S(2)}) %collective-permute-start.9) | collective-permute-done | bytes 786464 | tf_op jit(solution)/shard_map/ppermute | solution.py:15
  189.7 8.3 %convolution_bitcast_fusion = f32[2688,1536]{0,1:T(8,128)} fusion(bf16[256,2688]{1,0:T(8,128)(2,1)S(1)} %copy-done, bf16[256,1536]{0,1:T(8,128)(2,1)S(1)} %bitcast.54, bf16[256,1536]{0,1:T(8,128)(2,1)S(1)} %collective-permute-done.11, bf16[256,1536]{0,1:T(8,128)(2,1)S(1)} %collective-permute-done.10, bf16[256,1536]{0,1:T(8,128)(2,1)S(1)} %collective-permute-done.9, ...), kind=kOutput, calls=%fused_computation.8 | convolution fusion | flops 2117861376 | bytes 21823488 | tf_op jit(solution)/shard_map/dot_general | solution.py:79
  198.1 12.7 %reshape.90 = bf16[2688,1536]{1,0:T(8,128)(2,1)} reshape(bf16[32,84,1536]{2,1,0:T(8,128)(2,1)} %all-gather.3.cloned.1.call-done) | data formatting | bytes 16515072
  210.8 5.9 %convolution_convert_fusion = bf16[256,1536]{1,0:T(8,128)(2,1)S(1)} fusion(bf16[256,2688]{1,0:T(8,128)(2,1)S(1)} %copy-done, bf16[2688,1536]{1,0:T(8,128)(2,1)} %reshape.90), kind=kOutput, calls=%fused_computation.12 | convolution fusion | flops 2114322432 | bytes 10420224 | tf_op jit(solution)/shard_map/dot_general | solution.py:44
  220.5 7.0 %collective-permute-start.2 = (bf16[256,1536]{1,0:T(8,128)(2,1)S(1)}, bf16[256,1536]{1,0:T(8,128)(2,1)}, u32[]{:S(2)}, u32[]{:S(2)}) collective-permute-start(bf16[256,1536]{1,0:T(8,128)(2,1)S(1)} %convolution_convert_fusion), channel_id=1, source_target_pairs={{0,2},{1,3},{2,4},{3,5},{4,6},{5,7},{6,8},{7,9},{8,10},{9,11},{10,... | collective-permute-start | bytes 2359304 | tf_op jit(solution)/shard_map/ppermute | solution.py:15
  229.5 304.2 %all-reduce.4.cloned.1.call-done = f32[2688,1536]{0,1:T(8,128)} async-done(((f32[2688,1536]{0,1:T(8,128)}), f32[2688,1536]{0,1:T(8,128)}) %all-reduce.4.cloned.1.call-update) | async-done | bytes 16515088
  545.8 6.1 %copy.28 = bf16[1280,1536]{0,1:T(8,128)(2,1)} copy(bf16[1280,1536]{1,0:T(8,128)(2,1)} %constant_dynamic-update-slice_fusion) | data formatting | bytes 7864320 | tf_op jit(solution)/shard_map/concatenate | solution.py:52
  551.9 8.9 %convolution_convert_fusion.1 = bf16[12,128,2,256]{3,1,2,0:T(8,128)(2,1)S(1)} fusion(bf16[1280,12,128,1]{0,2,3,1:T(8,128)(2,1)} %bitcast.52, bf16[12,2,256,1280]{2,3,1,0:T(8,128)(2,1)} %divide_convert_fusion), kind=kOutput, calls=%fused_computation.13 | convolution fusion | flops 2014052352 | bytes 21233664 | tf_op jit(solution)/shard_map/kgtl,lkd->tkgd/dot_general | solution.py:27
  (41 shorter events, 35.5 us)
Async XLA Ops:
  7.2 182.6 %copy-start = (bf16[256,2688]{1,0:T(8,128)(2,1)S(1)}, bf16[256,2688]{1,0:T(8,128)(2,1)}, u32[]{:S(2)}) copy-start(bf16[256,2688]{1,0:T(8,128)(2,1)} %param.6) | copy-start | bytes 4128772
  7.2 190.9 %all-gather.3.cloned.1.call-start = ((), (), s32[]{:S(2)}) async-start(), calls=%async_computation | async-start | bytes 8921088 | tf_op jit(solution)/shard_map/all_gather | solution.py:46
  7.9 525.8 %all-reduce.4.cloned.1.call-start = ((), (), s32[]{:S(2)}) async-start(), calls=%async_computation.1 | async-start | bytes 33030144
  9.4 57.0 %collective-permute-start.4 = (bf16[256,1536]{0,1:T(8,128)(2,1)S(1)}, bf16[256,1536]{0,1:T(8,128)(2,1)}, u32[]{:S(2)}, u32[]{:S(2)}) collective-permute-start(bf16[256,1536]{0,1:T(8,128)(2,1)S(1)} %copy.29), channel_id=1, source_target_pairs={{0,4},{1,5},{2,6},{3,7},{4,8},{5,9},{6,10},{7,11},{8,12},{9,13},{1... | collective-permute-start | bytes 2359304 | tf_op jit(solution)/shard_map/ppermute | solution.py:15
  12.8 54.8 %collective-permute-start.5 = (bf16[256,1536]{0,1:T(8,128)(2,1)S(1)}, bf16[256,1536]{0,1:T(8,128)(2,1)}, u32[]{:S(2)}, u32[]{:S(2)}) collective-permute-start(bf16[256,1536]{0,1:T(8,128)(2,1)S(1)} %copy.29), channel_id=1, source_target_pairs={{0,3},{1,4},{2,5},{3,6},{4,7},{5,8},{6,9},{7,10},{8,11},{9,12},{10... | collective-permute-start | bytes 2359304 | tf_op jit(solution)/shard_map/ppermute | solution.py:15
  15.4 60.5 %collective-permute-start.6 = (bf16[256,1536]{0,1:T(8,128)(2,1)S(1)}, bf16[256,1536]{0,1:T(8,128)(2,1)}, u32[]{:S(2)}, u32[]{:S(2)}) collective-permute-start(bf16[256,1536]{0,1:T(8,128)(2,1)S(1)} %copy.29), channel_id=1, source_target_pairs={{0,2},{1,3},{2,4},{3,5},{4,6},{5,7},{6,8},{7,9},{8,10},{9,11},{10,... | collective-permute-start | bytes 2359304 | tf_op jit(solution)/shard_map/ppermute | solution.py:15
  18.8 73.1 %collective-permute-start.7 = (bf16[256,1536]{0,1:T(8,128)(2,1)S(1)}, bf16[256,1536]{0,1:T(8,128)(2,1)S(1)}, u32[]{:S(2)}, u32[]{:S(2)}) collective-permute-start(bf16[256,1536]{0,1:T(8,128)(2,1)S(1)} %copy.29), channel_id=1, source_target_pairs={{0,1},{1,2},{2,3},{3,4},{4,5},{5,6},{6,7},{7,8},{8,9},{9,10},{10,1... | collective-permute-start | bytes 2359304 | tf_op jit(solution)/shard_map/ppermute | solution.py:15
  92.0 1.9 copy-start.2
  112.2 17.1 %copy-start.1 = (bf16[256,3072]{0,1:T(8,128)(2,1)S(1)}, bf16[256,3072]{0,1:T(8,128)(2,1)}, u32[]{:S(2)}) copy-start(bf16[256,3072]{0,1:T(8,128)(2,1)} %copy.48) | copy-start | bytes 4718596
  138.3 19.9 %collective-permute-start.10 = (bf16[256,1536]{0,1:T(8,128)(2,1)S(1)}, bf16[256,1536]{0,1:T(8,128)(2,1)S(1)}, u32[]{:S(2)}, u32[]{:S(2)}) collective-permute-start(bf16[256,1536]{0,1:T(8,128)(2,1)S(1)} %bitcast.59), channel_id=1, source_target_pairs={{3,0},{4,1},{5,2},{6,3},{7,4},{8,5},{9,6},{10,7},{11,8},{12,9},{13... | collective-permute-start | bytes 2359304 | tf_op jit(solution)/shard_map/ppermute | solution.py:15
  140.2 30.7 %collective-permute-start.11 = (bf16[256,1536]{0,1:T(8,128)(2,1)S(1)}, bf16[256,1536]{0,1:T(8,128)(2,1)S(1)}, u32[]{:S(2)}, u32[]{:S(2)}) collective-permute-start(bf16[256,1536]{0,1:T(8,128)(2,1)S(1)} %bitcast.58), channel_id=1, source_target_pairs={{4,0},{5,1},{6,2},{7,3},{8,4},{9,5},{10,6},{11,7},{12,8},{13,9},{1... | collective-permute-start | bytes 2359304 | tf_op jit(solution)/shard_map/ppermute | solution.py:15
  142.2 39.1 %collective-permute-start.8 = (bf16[256,1536]{0,1:T(8,128)(2,1)S(1)}, bf16[256,1536]{0,1:T(8,128)(2,1)S(1)}, u32[]{:S(2)}, u32[]{:S(2)}) collective-permute-start(bf16[256,1536]{0,1:T(8,128)(2,1)S(1)} %bitcast.57), channel_id=1, source_target_pairs={{1,0},{2,1},{3,2},{4,3},{5,4},{6,5},{7,6},{8,7},{9,8},{10,9},{11,1... | collective-permute-start | bytes 2359304 | tf_op jit(solution)/shard_map/ppermute | solution.py:15
  147.1 42.6 %collective-permute-start.9 = (bf16[256,1536]{0,1:T(8,128)(2,1)S(1)}, bf16[256,1536]{0,1:T(8,128)(2,1)S(1)}, u32[]{:S(2)}, u32[]{:S(2)}) collective-permute-start(bf16[256,1536]{0,1:T(8,128)(2,1)S(1)} %bitcast.56), channel_id=1, source_target_pairs={{2,0},{3,1},{4,2},{5,3},{6,4},{7,5},{8,6},{9,7},{10,8},{11,9},{12,... | collective-permute-start | bytes 2359304 | tf_op jit(solution)/shard_map/ppermute | solution.py:15
  216.7 319.8 %collective-permute-start = (bf16[256,1536]{1,0:T(8,128)(2,1)S(1)}, bf16[256,1536]{1,0:T(8,128)(2,1)}, u32[]{:S(2)}, u32[]{:S(2)}) collective-permute-start(bf16[256,1536]{1,0:T(8,128)(2,1)S(1)} %convolution_convert_fusion), channel_id=1, source_target_pairs={{0,4},{1,5},{2,6},{3,7},{4,8},{5,9},{6,10},{7,11},{8,12},{9,13},{1... | collective-permute-start | bytes 2359304 | tf_op jit(solution)/shard_map/ppermute | solution.py:15
  218.6 319.9 %collective-permute-start.1 = (bf16[256,1536]{1,0:T(8,128)(2,1)S(1)}, bf16[256,1536]{1,0:T(8,128)(2,1)}, u32[]{:S(2)}, u32[]{:S(2)}) collective-permute-start(bf16[256,1536]{1,0:T(8,128)(2,1)S(1)} %convolution_convert_fusion), channel_id=1, source_target_pairs={{0,3},{1,4},{2,5},{3,6},{4,7},{5,8},{6,9},{7,10},{8,11},{9,12},{10... | collective-permute-start | bytes 2359304 | tf_op jit(solution)/shard_map/ppermute | solution.py:15
  220.5 320.1 %collective-permute-start.2 = (bf16[256,1536]{1,0:T(8,128)(2,1)S(1)}, bf16[256,1536]{1,0:T(8,128)(2,1)}, u32[]{:S(2)}, u32[]{:S(2)}) collective-permute-start(bf16[256,1536]{1,0:T(8,128)(2,1)S(1)} %convolution_convert_fusion), channel_id=1, source_target_pairs={{0,2},{1,3},{2,4},{3,5},{4,6},{5,7},{6,8},{7,9},{8,10},{9,11},{10,... | collective-permute-start | bytes 2359304 | tf_op jit(solution)/shard_map/ppermute | solution.py:15
  227.6 315.2 %collective-permute-start.3 = (bf16[256,1536]{1,0:T(8,128)(2,1)S(1)}, bf16[256,1536]{1,0:T(8,128)(2,1)}, u32[]{:S(2)}, u32[]{:S(2)}) collective-permute-start(bf16[256,1536]{1,0:T(8,128)(2,1)S(1)} %convolution_convert_fusion), channel_id=1, source_target_pairs={{0,1},{1,2},{2,3},{3,4},{4,5},{5,6},{6,7},{7,8},{8,9},{9,10},{10,1... | collective-permute-start | bytes 2359304 | tf_op jit(solution)/shard_map/ppermute | solution.py:15
Sparse Core Ops, SparseCore 0:
  10.9 112.3 all-gather.2
  198.2 335.4 all-reduce.3
where the time goes:
time: 573 us; the launch traced here: 569 us
  waiting for transfers between devices  403 us (70%)
  matrix products  49.9 us (9%)
  local copies, waits for them, and re-layouts  49.2 us (9%)
  starting transfers between devices  35.6 us (6%)
  other arithmetic  17.5 us (3%)
  between operations  14.3 us (2%)
    unnamed x3, waiting for transfers between devices  305 us
    ppermute x12, waiting for transfers between devices, passed_along(): return lax.ppermute(block, axis, route)  98 us
    ppermute x12, starting transfers between devices, passed_along(): return lax.ppermute(block, axis, route)  35.5 us
    unnamed x19, local copies, waits for them, and re-layouts  32.4 us
    sub x1, matrix products, attend(): weights = jnp.exp(scores - highest)  18.3 us
    convert_element_type x1, other arithmetic, attend(): (weights / jnp.sum(weights, axis=-1, keepdims=True)).astype(jnp.bfloat16)  17.1 us
  transfers between devices with their start and end apart: 14, of which 8 were waited for; matrix products, arithmetic and copies ran while one was open for 17% of the time, Pallas kernels for 0%

commit v1 on v0

--- a/solution.py
+++ b/solution.py
@@ -7,6 +7,7 @@
 
 HD = 128
 WINDOW = 1024
+GROUP = 8
 
 
 def passed_along(block, axis, distance):
@@ -31,6 +32,49 @@
     return (output, partial_value)
 
 
+def group_of(devices):
+    return math.gcd(devices, GROUP)
+
+
+def within_group(block, step):
+    devices = lax.axis_size("seq")
+    return lax.ppermute(block, "seq", [(i, i ^ step) for i in range(devices)])
+
+
+def hidden_exchange(hidden_rows):
+    devices = lax.axis_size("seq")
+    group = group_of(devices)
+    rank = lax.rem(lax.axis_index("seq"), group)
+    tokens, features = hidden_rows.shape
+    columns = hidden_rows.T.reshape(devices // group, group, features // devices, tokens)
+    received = []
+    for step in range(group):
+        block = lax.dynamic_index_in_dim(columns, rank ^ step, 1, keepdims=False)
+        received.append(within_group(block, step) if step else block)
+    return jnp.concatenate(received, axis=-1)
+
+
+def weight_gradient(hidden_sent, value_grad):
+    devices = lax.axis_size("seq")
+    group = group_of(devices)
+    groups = devices // group
+    received = [value_grad] + [within_group(value_grad, step) for step in range(1, group)]
+    terms = lax.dot_general(
+        hidden_sent,
+        jnp.concatenate(received, axis=0),
+        (((2,), (0,)), ((), ())),
+        preferred_element_type=jnp.float32,
+    )
+    here = lax.axis_index("seq") // group
+    total = lax.dynamic_index_in_dim(terms, here, 0, keepdims=False)
+    rounded = terms.astype(jnp.bfloat16)
+    for step in range(1, groups):
+        block = lax.dynamic_index_in_dim(rounded, lax.rem(here + step, groups), 0, keepdims=False)
+        route = [(i, (i + step * group) % devices) for i in range(devices)]
+        total = total + lax.ppermute(block, "seq", route).astype(jnp.float32)
+    return total
+
+
 def per_device(hidden_rows, value_weight, queries, key_rows, out_grad, segments):
     rows_here = hidden_rows.shape[0]
     kv_width = value_weight.shape[1]
@@ -40,9 +84,9 @@
     key_span = (blocks_back + 1) * rows_here
     padding = blocks_back * rows_here
     scale = 1.0 / math.sqrt(HD)
-    columns = hidden_rows
+    hidden_sent = hidden_exchange(hidden_rows)
     values = jnp.dot(
-        columns,
+        hidden_rows,
         lax.all_gather(value_weight, "seq", axis=0, tiled=True),
         preferred_element_type=jnp.float32,
     ).astype(jnp.bfloat16)
@@ -74,15 +118,7 @@
         ]
         gathered = gathered + passed_along(portion, "seq", -offset).astype(jnp.float32)
     value_grad = gathered.astype(jnp.bfloat16)
-    columns = hidden_rows
-    weight_grad = lax.psum_scatter(
-        lax.dot_general(
-            columns, value_grad, (((0,), (0,)), ((), ())), preferred_element_type=jnp.float32
-        ),
-        "seq",
-        scatter_dimension=0,
-        tiled=True,
-    )
+    weight_grad = weight_gradient(hidden_sent, value_grad)
     return (attention, weight_grad)
 
 

time: 573 us -> 448 us (0.78)
  waiting for transfers between devices: 403 us -> 255 us
  starting transfers between devices: 35.6 us -> 49.8 us
  local copies, waits for them, and re-layouts: 49.2 us -> 60.4 us
    unnamed x3 -> x1, waiting for transfers between devices: 305 us -> 0.68 us
    ppermute x0 -> x17, waiting for transfers between devices: none -> 88.9 us  [the longest x14 72.9 us: within_group(): return lax.ppermute(block, 'seq', [(i, i ^ step) for i in range(devices)])]
    ppermute x12, waiting for transfers between devices: 98 us -> 166 us  [passed_along(): return lax.ppermute(block, axis, route)]
    ppermute x0 -> x17, starting transfers between devices: none -> 16 us  [the longest x14 12.7 us: within_group(): return lax.ppermute(block, 'seq', [(i, i ^ step) for i in range(devices)])]
    slice x1 -> x5, local copies, waits for them, and re-layouts: 0.46 us -> 8.5 us  [per_device(): partial_value[(blocks_back - offset) * rows_here:(blocks_back - offset +...]
    unnamed x19 -> x38, local copies, waits for them, and re-layouts: 32.4 us -> 30 us
  transfers between devices with their start and end apart: 14 -> 30, of which waited for: 8 -> 15; matrix products, arithmetic and copies ran while one was open for 17% -> 20% of each run, Pallas kernels for 0% -> 0%
where the time goes in v1:
time: 448 us; the launch traced here: 447 us
  waiting for transfers between devices  255 us (57%)
  local copies, waits for them, and re-layouts  60.4 us (13%)
  starting transfers between devices  49.8 us (11%)
  matrix products  44.5 us (10%)
  other arithmetic  22.1 us (5%)
  between operations  14.5 us (3%)
    ppermute x12, waiting for transfers between devices, passed_along(): return lax.ppermute(block, axis, route)  166 us
    ppermute x14, waiting for transfers between devices, within_group(): return lax.ppermute(block, 'seq', [(i, i ^ step) for i in range(devices)])  72.9 us
    ppermute x12, starting transfers between devices, passed_along(): return lax.ppermute(block, axis, route)  33.8 us
    unnamed x38, local copies, waits for them, and re-layouts  30 us
    sub x1, matrix products, attend(): weights = jnp.exp(scores - highest)  17.5 us
    convert_element_type x1, other arithmetic, attend(): (weights / jnp.sum(weights, axis=-1, keepdims=True)).astype(jnp.bfloat16)  17.1 us
    ppermute x3, waiting for transfers between devices, weight_gradient(): total = total + lax.ppermute(block, 'seq', route).astype(jnp.float32)  16 us
    ppermute x14, starting transfers between devices, within_group(): return lax.ppermute(block, 'seq', [(i, i ^ step) for i in range(devices)])  12.7 us
  transfers between devices with their start and end apart: 30, of which 15 were waited for; matrix products, arithmetic and copies ran while one was open for 20% of the time, Pallas kernels for 0%

profile of v1, /device:TPU:16, one launch (start us, length us, event | category | flops | bytes accessed | tf_op | source)
XLA Modules:
  0.0 446.8 jit_solution(1853120818805046738)
XLA Ops:
  24.3 5.0 %reshape.89 = bf16[256,12,2,128]{3,2,1,0:T(2,128)(2,1)} reshape(bf16[256,3072]{1,0:T(8,128)(2,1)} %param.8) | data formatting | bytes 3145728 | tf_op jit(solution)/shard_map/reshape | solution.py:107
  33.0 34.5 %collective-permute-done.4 = bf16[256,1536]{0,1:T(8,128)(2,1)} collective-permute-done((bf16[256,1536]{0,1:T(8,128)(2,1)}, bf16[256,1536]{0,1:T(8,128)(2,1)}, u32[]{:S(2)}, u32[]{:S(2)}) %collective-permute-start.4) | collective-permute-done | bytes 786464 | tf_op jit(solution)/shard_map/ppermute | solution.py:16
  71.8 5.1 %collective-permute-done.6 = bf16[256,1536]{0,1:T(8,128)(2,1)} collective-permute-done((bf16[256,1536]{0,1:T(8,128)(2,1)}, bf16[256,1536]{0,1:T(8,128)(2,1)}, u32[]{:S(2)}, u32[]{:S(2)}) %collective-permute-start.6) | collective-permute-done | bytes 786464 | tf_op jit(solution)/shard_map/ppermute | solution.py:16
  79.0 14.0 %collective-permute-done.7 = bf16[256,1536]{0,1:T(8,128)(2,1)} collective-permute-done((bf16[256,1536]{0,1:T(8,128)(2,1)}, bf16[256,1536]{0,1:T(8,128)(2,1)}, u32[]{:S(2)}, u32[]{:S(2)}) %collective-permute-start.7) | collective-permute-done | bytes 786464 | tf_op jit(solution)/shard_map/ppermute | solution.py:16
  97.3 17.5 %fusion.26 = (f32[12,2,256]{2,1,0:T(2,128)S(1)}, f32[12,2,256,1280]{2,3,1,0:T(8,128)}) fusion(pred[256,1280]{0,1:T(8,128)(4,1)S(1)} %fusion.20, bf16[1280,12,128,1]{0,2,3,1:T(8,128)(2,1)} %bitcast.35, bf16[256,12,2,128]{3,2,1,0:T(2,128)(2,1)S(1)} %copy-done.3), kind=kOutput, calls=%fused_computation.69 | convolution fusion | flops 2044724480 | bytes 37314560 | tf_op jit(solution)/shard_map/sub | solution.py:26
  114.8 17.1 %divide_convert_fusion = bf16[12,2,256,1280]{2,3,1,0:T(8,128)(2,1)} fusion(f32[12,2,256,1280]{2,3,1,0:T(8,128)} %get-tuple-element.26, f32[12,2,256]{2,1,0:T(2,128)S(1)} %get-tuple-element.25), kind=kLoop, calls=%fused_computation.2 | loop fusion | flops 15728640 | bytes 47210496 | tf_op jit(solution)/shard_map/convert_element_type | solution.py:27
  131.9 8.6 %fusion.7 = bf16[1280,12,128]{0,2,1:T(8,128)(2,1)S(1)} fusion(bf16[12,2,256,1280]{2,3,1,0:T(8,128)(2,1)} %divide_convert_fusion, bf16[256,12,2,128]{0,3,2,1:T(8,128)(2,1)S(1)} %bitcast.89), kind=kOutput, calls=%fused_computation.11 | convolution fusion | flops 2015232000 | bytes 21233664 | tf_op jit(solution)/shard_map/kgtl,tkgd->lkd/dot_general | solution.py:29
  155.1 4.0 collective-permute-start.18
  163.2 29.8 %collective-permute-done.16 = bf16[256,1536]{1,0:T(8,128)(2,1)} collective-permute-done((bf16[256,1536]{1,0:T(8,128)(2,1)}, bf16[256,1536]{1,0:T(8,128)(2,1)}, u32[]{:S(2)}, u32[]{:S(2)}) %collective-permute-start.16) | collective-permute-done | bytes 786464 | tf_op jit(solution)/shard_map/ppermute | solution.py:16
  193.1 16.8 %collective-permute-done.17 = bf16[256,1536]{1,0:T(8,128)(2,1)} collective-permute-done((bf16[256,1536]{1,0:T(8,128)(2,1)}, bf16[256,1536]{1,0:T(8,128)(2,1)}, u32[]{:S(2)}, u32[]{:S(2)}) %collective-permute-start.17) | collective-permute-done | bytes 786464 | tf_op jit(solution)/shard_map/ppermute | solution.py:16
  209.9 12.6 %collective-permute-done.18 = bf16[256,1536]{1,0:T(8,128)(2,1)} collective-permute-done((bf16[256,1536]{1,0:T(8,128)(2,1)}, bf16[256,1536]{1,0:T(8,128)(2,1)}, u32[]{:S(2)}, u32[]{:S(2)}) %collective-permute-start.18) | collective-permute-done | bytes 786464 | tf_op jit(solution)/shard_map/ppermute | solution.py:16
  237.6 18.4 %collective-permute-done.14 = bf16[4,84,256]{2,1,0:T(8,128)(2,1)S(1)} collective-permute-done((bf16[4,84,256]{2,1,0:T(8,128)(2,1)S(1)}, bf16[4,84,256]{2,1,0:T(8,128)(2,1)S(1)}, u32[]{:S(2)}, u32[]{:S(2)}) %collective-permute-start.14) | collective-permute-done | bytes 172064 | tf_op jit(solution)/shard_map/ppermute | solution.py:41
  260.3 12.0 %collective-permute-done.21 = bf16[256,1536]{1,0:T(8,128)(2,1)S(1)} collective-permute-done((bf16[256,1536]{1,0:T(8,128)(2,1)S(1)}, bf16[256,1536]{1,0:T(8,128)(2,1)S(1)}, u32[]{:S(2)}, u32[]{:S(2)}) %collective-permute-start.21) | collective-permute-done | bytes 786464 | tf_op jit(solution)/shard_map/ppermute | solution.py:41
  272.4 36.6 %collective-permute-done.23 = bf16[256,1536]{1,0:T(8,128)(2,1)S(1)} collective-permute-done((bf16[256,1536]{1,0:T(8,128)(2,1)S(1)}, bf16[256,1536]{1,0:T(8,128)(2,1)S(1)}, u32[]{:S(2)}, u32[]{:S(2)}) %collective-permute-start.23) | collective-permute-done | bytes 786464 | tf_op jit(solution)/shard_map/ppermute | solution.py:41
  313.1 12.6 %reshape.94 = bf16[2688,1536]{1,0:T(8,128)(2,1)} reshape(bf16[32,84,1536]{2,1,0:T(8,128)(2,1)} %all-gather.3.cloned.1.call-done) | data formatting | bytes 16515072
  325.7 5.7 %convolution_convert_fusion = bf16[256,1536]{1,0:T(8,128)(2,1)S(1)} fusion(bf16[256,2688]{1,0:T(8,128)(2,1)S(1)} %copy-done.4, bf16[2688,1536]{1,0:T(8,128)(2,1)} %reshape.94), kind=kOutput, calls=%fused_computation.13 | convolution fusion | flops 2114322432 | bytes 10420224 | tf_op jit(solution)/shard_map/dot_general | solution.py:88
  331.4 4.1 collective-permute-start
  341.5 16.0 %collective-permute-done.26 = bf16[84,1536]{1,0:T(8,128)(2,1)S(1)} collective-permute-done((bf16[84,1536]{1,0:T(8,128)(2,1)}, bf16[84,1536]{1,0:T(8,128)(2,1)S(1)}, u32[]{:S(2)}, u32[]{:S(2)}) %collective-permute-start.26) | collective-permute-done | bytes 258080 | tf_op jit(solution)/shard_map/ppermute | solution.py:74
  357.5 3.9 collective-permute-start.2
  366.3 24.5 %collective-permute-done.1 = bf16[256,1536]{1,0:T(8,128)(2,1)S(1)} collective-permute-done((bf16[256,1536]{1,0:T(8,128)(2,1)S(1)}, bf16[256,1536]{1,0:T(8,128)(2,1)S(1)}, u32[]{:S(2)}, u32[]{:S(2)}) %collective-permute-start.1) | collective-permute-done | bytes 786464 | tf_op jit(solution)/shard_map/ppermute | solution.py:16
  391.7 21.9 %collective-permute-done.2 = bf16[256,1536]{1,0:T(8,128)(2,1)S(1)} collective-permute-done((bf16[256,1536]{1,0:T(8,128)(2,1)S(1)}, bf16[256,1536]{1,0:T(8,128)(2,1)S(1)}, u32[]{:S(2)}, u32[]{:S(2)}) %collective-permute-start.2) | collective-permute-done | bytes 786464 | tf_op jit(solution)/shard_map/ppermute | solution.py:16
  414.5 6.7 %collective-permute-done.3 = bf16[256,1536]{1,0:T(8,128)(2,1)S(1)} collective-permute-done((bf16[256,1536]{1,0:T(8,128)(2,1)S(1)}, bf16[256,1536]{1,0:T(8,128)(2,1)S(1)}, u32[]{:S(2)}, u32[]{:S(2)}) %collective-permute-start.3) | collective-permute-done | bytes 786464 | tf_op jit(solution)/shard_map/ppermute | solution.py:16
  423.1 6.2 %copy.45 = bf16[1280,1536]{0,1:T(8,128)(2,1)} copy(bf16[1280,1536]{1,0:T(8,128)(2,1)} %constant_dynamic-update-slice_fusion) | data formatting | bytes 7864320 | tf_op jit(solution)/shard_map/concatenate | solution.py:96
  429.3 8.9 %convolution_convert_fusion.1 = bf16[12,128,2,256]{3,1,2,0:T(8,128)(2,1)S(1)} fusion(bf16[1280,12,128,1]{0,2,3,1:T(8,128)(2,1)} %bitcast.83, bf16[12,2,256,1280]{2,3,1,0:T(8,128)(2,1)} %divide_convert_fusion), kind=kOutput, calls=%fused_computation.14 | convolution fusion | flops 2014052352 | bytes 21233664 | tf_op jit(solution)/shard_map/kgtl,lkd->tkgd/dot_general | solution.py:28
  (105 shorter events, 89.8 us)
Async XLA Ops:
  7.2 305.9 %all-gather.3.cloned.1.call-start = ((), (), s32[]{:S(2)}) async-start(), calls=%async_computation | async-start | bytes 8921088 | tf_op jit(solution)/shard_map/all_gather | solution.py:90
  10.2 57.3 %collective-permute-start.4 = (bf16[256,1536]{0,1:T(8,128)(2,1)}, bf16[256,1536]{0,1:T(8,128)(2,1)}, u32[]{:S(2)}, u32[]{:S(2)}) collective-permute-start(bf16[256,1536]{0,1:T(8,128)(2,1)} %copy.46), channel_id=1, source_target_pairs={{0,4},{1,5},{2,6},{3,7},{4,8},{5,9},{6,10},{7,11},{8,12},{9,13},{1... | collective-permute-start | bytes 2359304 | tf_op jit(solution)/shard_map/ppermute | solution.py:16
  13.6 56.0 %collective-permute-start.5 = (bf16[256,1536]{0,1:T(8,128)(2,1)}, bf16[256,1536]{0,1:T(8,128)(2,1)}, u32[]{:S(2)}, u32[]{:S(2)}) collective-permute-start(bf16[256,1536]{0,1:T(8,128)(2,1)} %copy.46), channel_id=1, source_target_pairs={{0,3},{1,4},{2,5},{3,6},{4,7},{5,8},{6,9},{7,10},{8,11},{9,12},{10... | collective-permute-start | bytes 2359304 | tf_op jit(solution)/shard_map/ppermute | solution.py:16
  16.2 60.7 %collective-permute-start.6 = (bf16[256,1536]{0,1:T(8,128)(2,1)}, bf16[256,1536]{0,1:T(8,128)(2,1)}, u32[]{:S(2)}, u32[]{:S(2)}) collective-permute-start(bf16[256,1536]{0,1:T(8,128)(2,1)} %copy.46), channel_id=1, source_target_pairs={{0,2},{1,3},{2,4},{3,5},{4,6},{5,7},{6,8},{7,9},{8,10},{9,11},{10,... | collective-permute-start | bytes 2359304 | tf_op jit(solution)/shard_map/ppermute | solution.py:16
  19.6 73.4 %collective-permute-start.7 = (bf16[256,1536]{0,1:T(8,128)(2,1)}, bf16[256,1536]{0,1:T(8,128)(2,1)}, u32[]{:S(2)}, u32[]{:S(2)}) collective-permute-start(bf16[256,1536]{0,1:T(8,128)(2,1)} %copy.46), channel_id=1, source_target_pairs={{0,1},{1,2},{2,3},{3,4},{4,5},{5,6},{6,7},{7,8},{8,9},{9,10},{10,1... | collective-permute-start | bytes 2359304 | tf_op jit(solution)/shard_map/ppermute | solution.py:16
  148.6 44.4 %collective-permute-start.16 = (bf16[256,1536]{1,0:T(8,128)(2,1)}, bf16[256,1536]{1,0:T(8,128)(2,1)}, u32[]{:S(2)}, u32[]{:S(2)}) collective-permute-start(bf16[256,1536]{1,0:T(8,128)(2,1)} %copy.59), channel_id=1, source_target_pairs={{2,0},{3,1},{4,2},{5,3},{6,4},{7,5},{8,6},{9,7},{10,8},{11,9},{12,... | collective-permute-start | bytes 2359304 | tf_op jit(solution)/shard_map/ppermute | solution.py:16
  151.9 58.0 %collective-permute-start.17 = (bf16[256,1536]{1,0:T(8,128)(2,1)}, bf16[256,1536]{1,0:T(8,128)(2,1)}, u32[]{:S(2)}, u32[]{:S(2)}) collective-permute-start(bf16[256,1536]{1,0:T(8,128)(2,1)} %copy.60), channel_id=1, source_target_pairs={{3,0},{4,1},{5,2},{6,3},{7,4},{8,5},{9,6},{10,7},{11,8},{12,9},{13... | collective-permute-start | bytes 2359304 | tf_op jit(solution)/shard_map/ppermute | solution.py:16
  155.1 67.4 %collective-permute-start.18 = (bf16[256,1536]{1,0:T(8,128)(2,1)}, bf16[256,1536]{1,0:T(8,128)(2,1)}, u32[]{:S(2)}, u32[]{:S(2)}) collective-permute-start(bf16[256,1536]{1,0:T(8,128)(2,1)} %copy.61), channel_id=1, source_target_pairs={{4,0},{5,1},{6,2},{7,3},{8,4},{9,5},{10,6},{11,7},{12,8},{13,9},{1... | collective-permute-start | bytes 2359304 | tf_op jit(solution)/shard_map/ppermute | solution.py:16
  160.1 64.8 %collective-permute-start.8 = (bf16[4,84,256]{2,1,0:T(8,128)(2,1)}, bf16[4,84,256]{2,1,0:T(8,128)(2,1)S(1)}, u32[]{:S(2)}, u32[]{:S(2)}) collective-permute-start(bf16[4,84,256]{2,1,0:T(8,128)(2,1)} %get-tuple-element.21), channel_id=1, source_target_pairs={{0,1},{1,0},{2,3},{3,2},{4,5},{5,4},{6,7},{7,6},{8,9},{9,8},{10,11... | collective-permute-start | bytes 516104 | tf_op jit(solution)/shard_map/ppermute | solution.py:41
  162.6 66.1 %collective-permute-start.9 = (bf16[4,84,256]{2,1,0:T(8,128)(2,1)}, bf16[4,84,256]{2,1,0:T(8,128)(2,1)S(1)}, u32[]{:S(2)}, u32[]{:S(2)}) collective-permute-start(bf16[4,84,256]{2,1,0:T(8,128)(2,1)} %get-tuple-element.20), channel_id=1, source_target_pairs={{0,2},{1,3},{2,0},{3,1},{4,6},{5,7},{6,4},{7,5},{8,10},{9,11},{10,... | collective-permute-start | bytes 516104 | tf_op jit(solution)/shard_map/ppermute | solution.py:41
  193.1 35.7 %collective-permute-start.10 = (bf16[4,84,256]{2,1,0:T(8,128)(2,1)}, bf16[4,84,256]{2,1,0:T(8,128)(2,1)S(1)}, u32[]{:S(2)}, u32[]{:S(2)}) collective-permute-start(bf16[4,84,256]{2,1,0:T(8,128)(2,1)} %get-tuple-element.19), channel_id=1, source_target_pairs={{0,3},{1,2},{2,1},{3,0},{4,7},{5,6},{6,5},{7,4},{8,11},{9,10},{10,... | collective-permute-start | bytes 516104 | tf_op jit(solution)/shard_map/ppermute | solution.py:41
  224.8 32.4 %collective-permute-start.19 = (bf16[256,1536]{1,0:T(8,128)(2,1)S(1)}, bf16[256,1536]{1,0:T(8,128)(2,1)S(1)}, u32[]{:S(2)}, u32[]{:S(2)}) collective-permute-start(bf16[256,1536]{1,0:T(8,128)(2,1)S(1)} %get-tuple-element.9), channel_id=1, source_target_pairs={{0,1},{1,0},{2,3},{3,2},{4,5},{5,4},{6,7},{7,6},{8,9},{9,8},{10,11... | collective-permute-start | bytes 2359304 | tf_op jit(solution)/shard_map/ppermute | solution.py:41
  228.8 28.8 %collective-permute-start.20 = (bf16[256,1536]{1,0:T(8,128)(2,1)S(1)}, bf16[256,1536]{1,0:T(8,128)(2,1)S(1)}, u32[]{:S(2)}, u32[]{:S(2)}) collective-permute-start(bf16[256,1536]{1,0:T(8,128)(2,1)S(1)} %get-tuple-element.9), channel_id=1, source_target_pairs={{0,2},{1,3},{2,0},{3,1},{4,6},{5,7},{6,4},{7,5},{8,10},{9,11},{10,... | collective-permute-start | bytes 2359304 | tf_op jit(solution)/shard_map/ppermute | solution.py:41
  230.2 25.8 %collective-permute-start.14 = (bf16[4,84,256]{2,1,0:T(8,128)(2,1)S(1)}, bf16[4,84,256]{2,1,0:T(8,128)(2,1)S(1)}, u32[]{:S(2)}, u32[]{:S(2)}) collective-permute-start(bf16[4,84,256]{2,1,0:T(8,128)(2,1)S(1)} %get-tuple-element.15), channel_id=1, source_target_pairs={{0,7},{1,6},{2,5},{3,4},{4,3},{5,2},{6,1},{7,0},{8,15},{9,14},{10,... | collective-permute-start | bytes 516104 | tf_op jit(solution)/shard_map/ppermute | solution.py:41
  234.9 37.4 %collective-permute-start.21 = (bf16[256,1536]{1,0:T(8,128)(2,1)S(1)}, bf16[256,1536]{1,0:T(8,128)(2,1)S(1)}, u32[]{:S(2)}, u32[]{:S(2)}) collective-permute-start(bf16[256,1536]{1,0:T(8,128)(2,1)S(1)} %get-tuple-element.9), channel_id=1, source_target_pairs={{0,3},{1,2},{2,1},{3,0},{4,7},{5,6},{6,5},{7,4},{8,11},{9,10},{10,... | collective-permute-start | bytes 2359304 | tf_op jit(solution)/shard_map/ppermute | solution.py:41
  237.1 35.3 %collective-permute-start.22 = (bf16[256,1536]{1,0:T(8,128)(2,1)S(1)}, bf16[256,1536]{1,0:T(8,128)(2,1)S(1)}, u32[]{:S(2)}, u32[]{:S(2)}) collective-permute-start(bf16[256,1536]{1,0:T(8,128)(2,1)S(1)} %get-tuple-element.9), channel_id=1, source_target_pairs={{0,4},{1,5},{2,6},{3,7},{4,0},{5,1},{6,2},{7,3},{8,12},{9,13},{10,... | collective-permute-start | bytes 2359304 | tf_op jit(solution)/shard_map/ppermute | solution.py:41
  256.0 53.0 %collective-permute-start.23 = (bf16[256,1536]{1,0:T(8,128)(2,1)S(1)}, bf16[256,1536]{1,0:T(8,128)(2,1)S(1)}, u32[]{:S(2)}, u32[]{:S(2)}) collective-permute-start(bf16[256,1536]{1,0:T(8,128)(2,1)S(1)} %get-tuple-element.9), channel_id=1, source_target_pairs={{0,5},{1,4},{2,7},{3,6},{4,1},{5,0},{6,3},{7,2},{8,13},{9,12},{10,... | collective-permute-start | bytes 2359304 | tf_op jit(solution)/shard_map/ppermute | solution.py:41
  257.2 51.8 %collective-permute-start.24 = (bf16[256,1536]{1,0:T(8,128)(2,1)S(1)}, bf16[256,1536]{1,0:T(8,128)(2,1)S(1)}, u32[]{:S(2)}, u32[]{:S(2)}) collective-permute-start(bf16[256,1536]{1,0:T(8,128)(2,1)S(1)} %get-tuple-element.9), channel_id=1, source_target_pairs={{0,6},{1,7},{2,4},{3,5},{4,2},{5,3},{6,0},{7,1},{8,14},{9,15},{10,... | collective-permute-start | bytes 2359304 | tf_op jit(solution)/shard_map/ppermute | solution.py:41
  257.6 51.5 %collective-permute-start.25 = (bf16[256,1536]{1,0:T(8,128)(2,1)S(1)}, bf16[256,1536]{1,0:T(8,128)(2,1)S(1)}, u32[]{:S(2)}, u32[]{:S(2)}) collective-permute-start(bf16[256,1536]{1,0:T(8,128)(2,1)S(1)} %get-tuple-element.9), channel_id=1, source_target_pairs={{0,7},{1,6},{2,5},{3,4},{4,3},{5,2},{6,1},{7,0},{8,15},{9,14},{10,... | collective-permute-start | bytes 2359304 | tf_op jit(solution)/shard_map/ppermute | solution.py:41
  331.4 34.0 %collective-permute-start = (bf16[256,1536]{1,0:T(8,128)(2,1)S(1)}, bf16[256,1536]{1,0:T(8,128)(2,1)S(1)}, u32[]{:S(2)}, u32[]{:S(2)}) collective-permute-start(bf16[256,1536]{1,0:T(8,128)(2,1)S(1)} %convolution_convert_fusion), channel_id=1, source_target_pairs={{0,4},{1,5},{2,6},{3,7},{4,8},{5,9},{6,10},{7,11},{8,12},{9,13},{1... | collective-permute-start | bytes 2359304 | tf_op jit(solution)/shard_map/ppermute | solution.py:16
  338.2 25.1 %collective-permute-start.28 = (bf16[84,1536]{1,0:T(8,128)(2,1)S(1)}, bf16[84,1536]{1,0:T(8,128)(2,1)}, u32[]{:S(2)}, u32[]{:S(2)}) collective-permute-start(bf16[84,1536]{1,0:T(8,128)(2,1)S(1)} %get-tuple-element.23), channel_id=1, source_target_pairs={{0,24},{1,25},{2,26},{3,27},{4,28},{5,29},{6,30},{7,31},{8,0},{9,1... | collective-permute-start | bytes 774152 | tf_op jit(solution)/shard_map/ppermute | solution.py:74
  339.6 51.2 %collective-permute-start.1 = (bf16[256,1536]{1,0:T(8,128)(2,1)S(1)}, bf16[256,1536]{1,0:T(8,128)(2,1)S(1)}, u32[]{:S(2)}, u32[]{:S(2)}) collective-permute-start(bf16[256,1536]{1,0:T(8,128)(2,1)S(1)} %convolution_convert_fusion), channel_id=1, source_target_pairs={{0,3},{1,4},{2,5},{3,6},{4,7},{5,8},{6,9},{7,10},{8,11},{9,12},{10... | collective-permute-start | bytes 2359304 | tf_op jit(solution)/shard_map/ppermute | solution.py:16
  357.5 56.1 %collective-permute-start.2 = (bf16[256,1536]{1,0:T(8,128)(2,1)S(1)}, bf16[256,1536]{1,0:T(8,128)(2,1)S(1)}, u32[]{:S(2)}, u32[]{:S(2)}) collective-permute-start(bf16[256,1536]{1,0:T(8,128)(2,1)S(1)} %convolution_convert_fusion), channel_id=1, source_target_pairs={{0,2},{1,3},{2,4},{3,5},{4,6},{5,7},{6,8},{7,9},{8,10},{9,11},{10,... | collective-permute-start | bytes 2359304 | tf_op jit(solution)/shard_map/ppermute | solution.py:16
  361.4 59.8 %collective-permute-start.3 = (bf16[256,1536]{1,0:T(8,128)(2,1)S(1)}, bf16[256,1536]{1,0:T(8,128)(2,1)S(1)}, u32[]{:S(2)}, u32[]{:S(2)}) collective-permute-start(bf16[256,1536]{1,0:T(8,128)(2,1)S(1)} %convolution_convert_fusion), channel_id=1, source_target_pairs={{0,1},{1,2},{2,3},{3,4},{4,5},{5,6},{6,7},{7,8},{8,9},{9,10},{10,1... | collective-permute-start | bytes 2359304 | tf_op jit(solution)/shard_map/ppermute | solution.py:16
  (13 other events, 363.9 us)
Sparse Core Ops, SparseCore 0:
  10.9 113.3 all-gather.2

commit v2 on v1

v2 whole, which is shorter than its diff:
```python
import math

import jax
import jax.numpy as jnp
from jax import lax
from jax.sharding import PartitionSpec as P

HD = 128
WINDOW = 1024
GROUP = 8


def passed_along(block, axis, distance):
    devices = range(lax.axis_size(axis))
    route = [(i - distance, i) for i in devices if i - distance in devices]
    return lax.ppermute(block, axis, route)


def within_group(block, step):
    devices = lax.axis_size("seq")
    return lax.ppermute(block, "seq", [(i, i ^ step) for i in range(devices)])


def window_of(block, pairs, odd):
    rows = block.shape[0]
    straight = [block] + [passed_along(block, "seq", 2 * k) for k in range(1, pairs + 1)]
    wanted = lax.dynamic_slice_in_dim(
        jnp.concatenate(straight, axis=0), odd * rows, pairs * rows, 0
    )
    swapped = within_group(wanted, 1)
    ordered = [block]
    for k in range(pairs):
        ordered = [straight[k + 1], swapped[k * rows : (k + 1) * rows]] + ordered
    return jnp.concatenate(ordered, axis=0)


def summed_back(partial_value, pairs, odd, rows):
    def term(distance):
        start = (2 * pairs - distance) * rows
        return partial_value[start : start + rows]

    swapped = within_group(
        jnp.concatenate([term(2 * k + 1) for k in range(pairs)], axis=0), 1
    ).astype(jnp.float32)
    zero = jnp.zeros((rows, partial_value.shape[1]), jnp.float32)
    pieces = [swapped[k * rows : (k + 1) * rows] for k in range(pairs)]
    sums = [
        term(2 * k).astype(jnp.float32) + jnp.where(odd == 1, before, after)
        for k, (before, after) in enumerate(zip([zero] + pieces, pieces + [zero]))
    ]
    total = sums[0]
    for k in range(1, pairs + 1):
        portion = sums[k].astype(jnp.bfloat16)
        total = total + passed_along(portion, "seq", -2 * k).astype(jnp.float32)
    return total.astype(jnp.bfloat16)


def attend(query_four, grad_four, key_three, allowed, scale):
    scores = (
        jnp.einsum("tkgd,lkd->kgtl", query_four, key_three, preferred_element_type=jnp.float32)
        * scale
    )
    scores = jnp.where(allowed[None, None], scores, -1e30)
    highest = jnp.max(scores, axis=-1, keepdims=True)
    weights = jnp.exp(scores - highest)
    probs = (weights / jnp.sum(weights, axis=-1, keepdims=True)).astype(jnp.bfloat16)
    partial_value = jnp.einsum(
        "kgtl,tkgd->lkd", probs, grad_four, preferred_element_type=jnp.float32
    )
    return (probs, partial_value)


def group_of(devices):
    return math.gcd(devices, GROUP)


def hidden_exchange(hidden_rows):
    devices = lax.axis_size("seq")
    group = group_of(devices)
    rank = lax.rem(lax.axis_index("seq"), group)
    tokens, features = hidden_rows.shape
    columns = hidden_rows.T.reshape(devices // group, group, features // devices, tokens)
    received = []
    for step in list(range(0, group, 2)) + list(range(1, group, 2)):
        block = lax.dynamic_index_in_dim(columns, rank ^ step, 1, keepdims=False)
        received.append(within_group(block, step) if step else block)
    return jnp.concatenate(received, axis=-1)


def weight_gradient(hidden_sent, value_grad):
    devices = lax.axis_size("seq")
    group = group_of(devices)
    groups = devices // group
    received = [value_grad] + [within_group(value_grad, step) for step in range(2, group, 2)]
    received = jnp.concatenate(received, axis=0)
    terms = jnp.zeros((), jnp.float32)
    half = received.shape[0]
    for start, block in ((0, received), (half, within_group(received, 1))):
        terms = terms + lax.dot_general(
            hidden_sent[:, :, start : start + half],
            block,
            (((2,), (0,)), ((), ())),
            preferred_element_type=jnp.float32,
        )
    here = lax.axis_index("seq") // group
    total = lax.dynamic_index_in_dim(terms, here, 0, keepdims=False)
    rounded = terms.astype(jnp.bfloat16)
    for step in range(1, groups):
        block = lax.dynamic_index_in_dim(rounded, lax.rem(here + step, groups), 0, keepdims=False)
        route = [(i, (i + step * group) % devices) for i in range(devices)]
        total = total + lax.ppermute(block, "seq", route).astype(jnp.float32)
    return total


def per_device(hidden_rows, value_weight, queries, key_rows, out_grad, segments):
    rows_here = hidden_rows.shape[0]
    kv_width = value_weight.shape[1]
    kv_heads = kv_width // HD
    group_size = queries.shape[1] // kv_width
    blocks_back = (WINDOW + rows_here - 2) // rows_here
    key_span = (blocks_back + 1) * rows_here
    padding = blocks_back * rows_here
    scale = 1.0 / math.sqrt(HD)
    values = jnp.dot(
        hidden_rows,
        lax.all_gather(value_weight, "seq", axis=0, tiled=True),
        preferred_element_type=jnp.float32,
    ).astype(jnp.bfloat16)
    pairs = blocks_back // 2
    odd = lax.rem(lax.axis_index("seq"), 2)
    key_window = window_of(key_rows, pairs, odd)
    key_window, hidden_later = lax.optimization_barrier((key_window, hidden_rows))
    hidden_sent = hidden_exchange(hidden_later)
    position = lax.axis_index("seq")
    segs_padded = jnp.concatenate([jnp.full((padding,), -1, jnp.int32), segments], axis=0)
    key_seg = lax.dynamic_slice_in_dim(segs_padded, position * rows_here, key_span, 0)
    query_seg = lax.dynamic_slice_in_dim(segments, position * rows_here, rows_here, 0)
    distance = (
        jnp.arange(rows_here, dtype=jnp.int32)[:, None]
        + padding
        - jnp.arange(key_span, dtype=jnp.int32)[None, :]
    )
    allowed = (distance >= 0) & (distance < WINDOW) & (query_seg[:, None] == key_seg[None, :])
    query_four = queries.reshape(rows_here, kv_heads, group_size, HD)
    grad_four = out_grad.reshape(rows_here, kv_heads, group_size, HD)
    key_three = key_window.reshape(key_span, kv_heads, HD)
    probs, partial_value = attend(query_four, grad_four, key_three, allowed, scale)
    partial_value = partial_value.reshape(key_span, kv_width).astype(jnp.bfloat16)
    value_grad = summed_back(partial_value, pairs, odd, rows_here)
    value_grad, values = lax.optimization_barrier((value_grad, values))
    weight_grad = weight_gradient(hidden_sent, value_grad)
    value_three = window_of(values, pairs, odd).reshape(key_span, kv_heads, HD)
    output = jnp.einsum("kgtl,lkd->tkgd", probs, value_three, preferred_element_type=jnp.float32)
    attention = output.reshape(rows_here, kv_width * group_size).astype(jnp.bfloat16)
    return (attention, weight_grad)


def solution(mesh):
    in_specs = (P("seq", None), P("seq", "wt"), P("seq", "wt"), P("seq", "wt"), P("seq", "wt"), P())
    out_specs = (P("seq", "wt"), P("seq", "wt"))
    return jax.shard_map(
        per_device, mesh=mesh, in_specs=in_specs, out_specs=out_specs, check_vma=False
    )
```

time: 448 us -> 346 us (0.77)
  waiting for transfers between devices: 255 us -> 159 us
  starting transfers between devices: 49.8 us -> 29.3 us
  other arithmetic: 22.1 us -> 36 us
    ppermute x12 -> x6, waiting for transfers between devices: 166 us -> 82.9 us  [passed_along(): return lax.ppermute(block, axis, route)]
    ppermute x12 -> x6, starting transfers between devices: 33.8 us -> 16.6 us  [passed_along(): return lax.ppermute(block, axis, route)]
    convert_element_type x1 -> x5, other arithmetic: 0.16 us -> 10 us  [the longest x1 3.21 us: summed_back(): return total.astype(jnp.bfloat16)]
    ppermute x14, waiting for transfers between devices: 72.9 us -> 65.3 us  [within_group(): return lax.ppermute(block, 'seq', [(i, i ^ step) for i in range(devices)])]
    slice x5 -> x3, local copies, waits for them, and re-layouts: 8.5 us -> 2.14 us  [term(): return partial_value[start:start + rows]]
    concatenate x0 -> x3, other arithmetic: none -> 6.34 us  [the longest x2 5.07 us: window_of(): jnp.concatenate(straight, axis=0)]
    convert_element_type x1 -> x3, local copies, waits for them, and re-layouts: 0.47 us -> 6.28 us  [summed_back(): term(2 * k).astype(jnp.float32) + jnp.where(odd == 1, before, after)]
    ppermute x3, waiting for transfers between devices: 16 us -> 10.3 us  [weight_gradient(): total = total + lax.ppermute(block, 'seq', route).astype(jnp.float32)]
  transfers between devices with their start and end apart: 30 -> 24, of which waited for: 15 -> 11; matrix products, arithmetic and copies ran while one was open for 20% -> 32% of each run, Pallas kernels for 0% -> 0%
where the time goes in v2:
time: 346 us; the launch traced here: 342 us
  waiting for transfers between devices  159 us (46%)
  local copies, waits for them, and re-layouts  56.1 us (16%)
  matrix products  47.7 us (14%)
  other arithmetic  36 us (10%)
  starting transfers between devices  29.3 us (8%)
  between operations  14.4 us (4%)
    ppermute x6, waiting for transfers between devices, passed_along(): return lax.ppermute(block, axis, route)  82.9 us
    ppermute x14, waiting for transfers between devices, within_group(): return lax.ppermute(block, 'seq', [(i, i ^ step) for i in range(devices)])  65.3 us
    unnamed x46, local copies, waits for them, and re-layouts  30.6 us
    sub x1, matrix products, attend(): weights = jnp.exp(scores - highest)  17.5 us
    convert_element_type x1, other arithmetic, attend(): (weights / jnp.sum(weights, axis=-1, keepdims=True)).astype(jnp.bfloat16)  17.3 us
    ppermute x6, starting transfers between devices, passed_along(): return lax.ppermute(block, axis, route)  16.6 us
    ppermute x14, starting transfers between devices, within_group(): return lax.ppermute(block, 'seq', [(i, i ^ step) for i in range(devices)])  10.3 us
    ppermute x3, waiting for transfers between devices, weight_gradient(): total = total + lax.ppermute(block, 'seq', route).astype(jnp.float32)  10.3 us
  transfers between devices with their start and end apart: 24, of which 11 were waited for; matrix products, arithmetic and copies ran while one was open for 32% of the time, Pallas kernels for 0%

profile of v2, /device:TPU:16, one launch (start us, length us, event | category | flops | bytes accessed | tf_op | source)
XLA Modules:
  0.0 342.0 jit_solution(9839820974360062953)
XLA Ops:
  8.6 3.4 %collective-permute-start = (bf16[256,1536]{0,1:T(8,128)(2,1)S(1)}, bf16[256,1536]{0,1:T(8,128)(2,1)S(1)}, u32[]{:S(2)}, u32[]{:S(2)}) collective-permute-start(bf16[256,1536]{0,1:T(8,128)(2,1)S(1)} %copy.45), channel_id=1, source_target_pairs={{0,4},{1,5},{2,6},{3,7},{4,8},{5,9},{6,10},{7,11},{8,12},{9,13},{1... | collective-permute-start | bytes 2359304 | tf_op jit(solution)/shard_map/ppermute | solution.py:16
  12.1 3.4 collective-permute-start.1
  15.5 32.1 %collective-permute-done = bf16[256,1536]{0,1:T(8,128)(2,1)S(1)} collective-permute-done((bf16[256,1536]{0,1:T(8,128)(2,1)S(1)}, bf16[256,1536]{0,1:T(8,128)(2,1)S(1)}, u32[]{:S(2)}, u32[]{:S(2)}) %collective-permute-start) | collective-permute-done | bytes 786464 | tf_op jit(solution)/shard_map/ppermute | solution.py:16
  47.6 12.2 %collective-permute-done.1 = bf16[256,1536]{0,1:T(8,128)(2,1)S(1)} collective-permute-done((bf16[256,1536]{0,1:T(8,128)(2,1)S(1)}, bf16[256,1536]{0,1:T(8,128)(2,1)S(1)}, u32[]{:S(2)}, u32[]{:S(2)}) %collective-permute-start.1) | collective-permute-done | bytes 786464 | tf_op jit(solution)/shard_map/ppermute | solution.py:16
  61.7 5.1 %reshape.92 = bf16[256,12,2,128]{3,2,1,0:T(2,128)(2,1)} reshape(bf16[256,3072]{1,0:T(8,128)(2,1)} %param.8) | data formatting | bytes 3145728 | tf_op jit(solution)/shard_map/reshape | solution.py:144
  75.0 17.5 %fusion.51 = (f32[12,2,256]{2,1,0:T(2,128)S(1)}, f32[12,2,256,1280]{2,3,1,0:T(8,128)}) fusion(pred[256,1280]{0,1:T(8,128)(4,1)S(1)} %fusion.29, bf16[1280,12,128,1]{0,2,3,1:T(8,128)(2,1)} %bitcast.98, bf16[256,12,2,128]{3,2,1,0:T(2,128)(2,1)S(1)} %copy-done.12), kind=kOutput, calls=%fused_computation.92 | convolution fusion | flops 2044724480 | bytes 37314560 | tf_op jit(solution)/shard_map/sub | solution.py:65
  92.5 17.3 %divide_convert_fusion = bf16[12,2,256,1280]{2,3,1,0:T(8,128)(2,1)} fusion(f32[12,2,256,1280]{2,3,1,0:T(8,128)} %get-tuple-element.35, f32[12,2,256]{2,1,0:T(2,128)S(1)} %get-tuple-element.34), kind=kLoop, calls=%fused_computation.2 | loop fusion | flops 15728640 | bytes 47210496 | tf_op jit(solution)/shard_map/convert_element_type | solution.py:66
  109.8 8.7 %fusion.5 = bf16[1280,12,128]{0,2,1:T(8,128)(2,1)S(1)} fusion(bf16[12,2,256,1280]{2,3,1,0:T(8,128)(2,1)} %divide_convert_fusion, bf16[256,12,2,128]{0,3,2,1:T(8,128)(2,1)S(1)} %bitcast.95), kind=kOutput, calls=%fused_computation.9 | convolution fusion | flops 2015232000 | bytes 21233664 | tf_op jit(solution)/shard_map/kgtl,tkgd->lkd/dot_general | solution.py:67
  139.4 22.0 %collective-permute-done.4 = bf16[256,1536]{1,0:T(8,128)(2,1)} collective-permute-done((bf16[256,1536]{1,0:T(8,128)(2,1)}, bf16[256,1536]{1,0:T(8,128)(2,1)}, u32[]{:S(2)}, u32[]{:S(2)}) %collective-permute-start.4) | collective-permute-done | bytes 786464 | tf_op jit(solution)/shard_map/ppermute | solution.py:16
  161.4 16.6 %collective-permute-done.5 = bf16[256,1536]{1,0:T(8,128)(2,1)} collective-permute-done((bf16[256,1536]{1,0:T(8,128)(2,1)}, bf16[256,1536]{1,0:T(8,128)(2,1)}, u32[]{:S(2)}, u32[]{:S(2)}) %collective-permute-start.5) | collective-permute-done | bytes 786464 | tf_op jit(solution)/shard_map/ppermute | solution.py:16
  178.0 3.2 add_convert_fusion
  181.2 12.6 %reshape.100 = bf16[2688,1536]{1,0:T(8,128)(2,1)} reshape(bf16[32,84,1536]{2,1,0:T(8,128)(2,1)} %all-gather.3.cloned.1.call-done) | data formatting | bytes 16515072
  193.7 5.8 %convolution_convert_fusion = bf16[256,1536]{1,0:T(8,128)(2,1)S(1)} fusion(bf16[256,2688]{1,0:T(8,128)(2,1)S(1)} %copy-done.13, bf16[2688,1536]{1,0:T(8,128)(2,1)} %reshape.100), kind=kOutput, calls=%fused_computation.16 | convolution fusion | flops 2114322432 | bytes 10420224 | tf_op jit(solution)/shard_map/dot_general | solution.py:124
  199.6 3.2 collective-permute-start.13
  204.3 3.9 %collective-permute-start.6 = (bf16[256,1536]{1,0:T(8,128)(2,1)S(1)}, bf16[256,1536]{1,0:T(8,128)(2,1)S(1)}, u32[]{:S(2)}, u32[]{:S(2)}) collective-permute-start(bf16[256,1536]{1,0:T(8,128)(2,1)S(1)} %convolution_convert_fusion), channel_id=1, source_target_pairs={{0,4},{1,5},{2,6},{3,7},{4,8},{5,9},{6,10},{7,11},{8,12},{9,13},{1... | collective-permute-start | bytes 2359304 | tf_op jit(solution)/shard_map/ppermute | solution.py:16
  211.1 8.9 %collective-permute-done.12 = bf16[256,1536]{1,0:T(8,128)(2,1)S(1)} collective-permute-done((bf16[256,1536]{1,0:T(8,128)(2,1)S(1)}, bf16[256,1536]{1,0:T(8,128)(2,1)S(1)}, u32[]{:S(2)}, u32[]{:S(2)}) %collective-permute-start.12) | collective-permute-done | bytes 786464 | tf_op jit(solution)/shard_map/ppermute | solution.py:21
  221.0 49.9 %collective-permute-done.13 = bf16[256,1536]{1,0:T(8,128)(2,1)S(1)} collective-permute-done((bf16[256,1536]{1,0:T(8,128)(2,1)S(1)}, bf16[256,1536]{1,0:T(8,128)(2,1)S(1)}, u32[]{:S(2)}, u32[]{:S(2)}) %collective-permute-start.13) | collective-permute-done | bytes 786464 | tf_op jit(solution)/shard_map/ppermute | solution.py:21
  272.8 3.2 fusion.16
  288.3 6.1 %copy.58 = bf16[1280,1536]{0,1:T(8,128)(2,1)} copy(bf16[1280,1536]{1,0:T(8,128)(2,1)} %constant_dynamic-update-slice_fusion.3) | data formatting | bytes 7864320 | tf_op jit(solution)/shard_map/concatenate | solution.py:34
  297.9 3.2 fusion.8
  301.0 4.0 %collective-permute-done.10 = bf16[4,84,256]{2,1,0:T(8,128)(2,1)S(1)} collective-permute-done((bf16[4,84,256]{2,1,0:T(8,128)(2,1)S(1)}, bf16[4,84,256]{2,1,0:T(8,128)(2,1)S(1)}, u32[]{:S(2)}, u32[]{:S(2)}) %collective-permute-start.10) | collective-permute-done | bytes 172064 | tf_op jit(solution)/shard_map/ppermute | solution.py:21
  306.2 4.7 %fusion.56 = (bf16[4,84,1536]{2,1,0:T(8,128)(2,1)S(1)}, f32[4,84,1536]{2,1,0:T(8,128)}) fusion(f32[4,84,1536]{2,1,0:T(8,128)S(1)} %fusion.8, bf16[1024,1536]{1,0:T(8,128)(2,1)} %constant_dynamic-update-slice_fusion.6, bf16[4,84,256]{2,1,0:T(8,128)(2,1)S(1)} %collective-permute-done.11, bf16[4,84,256]{2,1,0:T(8,128)(2,1)S(1)} %collective-permute-done.10, ...), kind=kOutput, calls=%fused_computation.93 | convolution fusion | flops 1060749312 | bytes 8994816 | tf_op jit(solution)/shard_map/dot_general | solution.py:99
  313.4 7.7 %convolution_convert_fusion.1 = bf16[12,128,2,256]{3,1,2,0:T(8,128)(2,1)S(1)} fusion(bf16[1280,12,128,1]{0,2,3,1:T(8,128)(2,1)S(1)} %bitcast.91, bf16[12,2,256,1280]{2,3,1,0:T(8,128)(2,1)} %divide_convert_fusion), kind=kOutput, calls=%fused_computation.23 | convolution fusion | flops 2014052352 | bytes 21233664 | tf_op jit(solution)/shard_map/kgtl,lkd->tkgd/dot_general | solution.py:153
  322.9 9.2 %collective-permute-done.20 = bf16[84,1536]{1,0:T(8,128)(2,1)S(1)} collective-permute-done((bf16[84,1536]{1,0:T(8,128)(2,1)S(1)}, bf16[84,1536]{1,0:T(8,128)(2,1)S(1)}, u32[]{:S(2)}, u32[]{:S(2)}) %collective-permute-start.20) | collective-permute-done | bytes 258080 | tf_op jit(solution)/shard_map/ppermute | solution.py:111
  (107 shorter events, 63.7 us)
Async XLA Ops:
  7.2 174.0 %all-gather.3.cloned.1.call-start = ((), (), s32[]{:S(2)}) async-start(), calls=%async_computation | async-start | bytes 8921088 | tf_op jit(solution)/shard_map/all_gather | solution.py:126
  8.6 39.0 %collective-permute-start = (bf16[256,1536]{0,1:T(8,128)(2,1)S(1)}, bf16[256,1536]{0,1:T(8,128)(2,1)S(1)}, u32[]{:S(2)}, u32[]{:S(2)}) collective-permute-start(bf16[256,1536]{0,1:T(8,128)(2,1)S(1)} %copy.45), channel_id=1, source_target_pairs={{0,4},{1,5},{2,6},{3,7},{4,8},{5,9},{6,10},{7,11},{8,12},{9,13},{1... | collective-permute-start | bytes 2359304 | tf_op jit(solution)/shard_map/ppermute | solution.py:16
  12.1 47.7 %collective-permute-start.1 = (bf16[256,1536]{0,1:T(8,128)(2,1)S(1)}, bf16[256,1536]{0,1:T(8,128)(2,1)S(1)}, u32[]{:S(2)}, u32[]{:S(2)}) collective-permute-start(bf16[256,1536]{0,1:T(8,128)(2,1)S(1)} %copy.45), channel_id=1, source_target_pairs={{0,2},{1,3},{2,4},{3,5},{4,6},{5,7},{6,8},{7,9},{8,10},{9,11},{10,... | collective-permute-start | bytes 2359304 | tf_op jit(solution)/shard_map/ppermute | solution.py:16
  61.7 8.3 %collective-permute-start.2 = (bf16[512,1536]{0,1:T(8,128)(2,1)}, bf16[512,1536]{0,1:T(8,128)(2,1)}, u32[]{:S(2)}, u32[]{:S(2)}) collective-permute-start(bf16[512,1536]{0,1:T(8,128)(2,1)} %fusion.18), channel_id=1, source_target_pairs={{0,1},{1,0},{2,3},{3,2},{4,5},{5,4},{6,7},{7,6},{8,9},{9,8},{10,11... | collective-permute-start | bytes 4718600 | tf_op jit(solution)/shard_map/ppermute | solution.py:21
  121.9 4.9 %collective-permute-start.3 = (bf16[512,1536]{1,0:T(8,128)(2,1)}, bf16[512,1536]{1,0:T(8,128)(2,1)}, u32[]{:S(2)}, u32[]{:S(2)}) collective-permute-start(bf16[512,1536]{1,0:T(8,128)(2,1)} %pad_maximum_fusion), channel_id=1, source_target_pairs={{0,1},{1,0},{2,3},{3,2},{4,5},{5,4},{6,7},{7,6},{8,9},{9,8},{10,11... | collective-permute-start | bytes 4718600 | tf_op jit(solution)/shard_map/ppermute | solution.py:21
  131.1 30.2 %collective-permute-start.4 = (bf16[256,1536]{1,0:T(8,128)(2,1)}, bf16[256,1536]{1,0:T(8,128)(2,1)}, u32[]{:S(2)}, u32[]{:S(2)}) collective-permute-start(bf16[256,1536]{1,0:T(8,128)(2,1)} %get-tuple-element.21), channel_id=1, source_target_pairs={{2,0},{3,1},{4,2},{5,3},{6,4},{7,5},{8,6},{9,7},{10,8},{11,9},{12,... | collective-permute-start | bytes 2359304 | tf_op jit(solution)/shard_map/ppermute | solution.py:16
  133.1 44.9 %collective-permute-start.5 = (bf16[256,1536]{1,0:T(8,128)(2,1)}, bf16[256,1536]{1,0:T(8,128)(2,1)}, u32[]{:S(2)}, u32[]{:S(2)}) collective-permute-start(bf16[256,1536]{1,0:T(8,128)(2,1)} %get-tuple-element.22), channel_id=1, source_target_pairs={{4,0},{5,1},{6,2},{7,3},{8,4},{9,5},{10,6},{11,7},{12,8},{13,9},{1... | collective-permute-start | bytes 2359304 | tf_op jit(solution)/shard_map/ppermute | solution.py:16
  199.6 20.5 %collective-permute-start.12 = (bf16[256,1536]{1,0:T(8,128)(2,1)S(1)}, bf16[256,1536]{1,0:T(8,128)(2,1)S(1)}, u32[]{:S(2)}, u32[]{:S(2)}) collective-permute-start(bf16[256,1536]{1,0:T(8,128)(2,1)S(1)} %copy-done.9), channel_id=1, source_target_pairs={{0,2},{1,3},{2,0},{3,1},{4,6},{5,7},{6,4},{7,5},{8,10},{9,11},{10,... | collective-permute-start | bytes 2359304 | tf_op jit(solution)/shard_map/ppermute | solution.py:21
  199.6 71.3 %collective-permute-start.13 = (bf16[256,1536]{1,0:T(8,128)(2,1)S(1)}, bf16[256,1536]{1,0:T(8,128)(2,1)S(1)}, u32[]{:S(2)}, u32[]{:S(2)}) collective-permute-start(bf16[256,1536]{1,0:T(8,128)(2,1)S(1)} %copy-done.9), channel_id=1, source_target_pairs={{0,4},{1,5},{2,6},{3,7},{4,0},{5,1},{6,2},{7,3},{8,12},{9,13},{10,... | collective-permute-start | bytes 2359304 | tf_op jit(solution)/shard_map/ppermute | solution.py:21
  202.9 69.0 %collective-permute-start.14 = (bf16[256,1536]{1,0:T(8,128)(2,1)S(1)}, bf16[256,1536]{1,0:T(8,128)(2,1)S(1)}, u32[]{:S(2)}, u32[]{:S(2)}) collective-permute-start(bf16[256,1536]{1,0:T(8,128)(2,1)S(1)} %copy-done.9), channel_id=1, source_target_pairs={{0,6},{1,7},{2,4},{3,5},{4,2},{5,3},{6,0},{7,1},{8,14},{9,15},{10,... | collective-permute-start | bytes 2359304 | tf_op jit(solution)/shard_map/ppermute | solution.py:21
  204.3 68.5 %collective-permute-start.6 = (bf16[256,1536]{1,0:T(8,128)(2,1)S(1)}, bf16[256,1536]{1,0:T(8,128)(2,1)S(1)}, u32[]{:S(2)}, u32[]{:S(2)}) collective-permute-start(bf16[256,1536]{1,0:T(8,128)(2,1)S(1)} %convolution_convert_fusion), channel_id=1, source_target_pairs={{0,4},{1,5},{2,6},{3,7},{4,8},{5,9},{6,10},{7,11},{8,12},{9,13},{1... | collective-permute-start | bytes 2359304 | tf_op jit(solution)/shard_map/ppermute | solution.py:16
  208.2 64.6 %collective-permute-start.7 = (bf16[256,1536]{1,0:T(8,128)(2,1)S(1)}, bf16[256,1536]{1,0:T(8,128)(2,1)S(1)}, u32[]{:S(2)}, u32[]{:S(2)}) collective-permute-start(bf16[256,1536]{1,0:T(8,128)(2,1)S(1)} %convolution_convert_fusion), channel_id=1, source_target_pairs={{0,2},{1,3},{2,4},{3,5},{4,6},{5,7},{6,8},{7,9},{8,10},{9,11},{10,... | collective-permute-start | bytes 2359304 | tf_op jit(solution)/shard_map/ppermute | solution.py:16
  272.8 25.1 %collective-permute-start.19 = (bf16[1024,1536]{1,0:T(8,128)(2,1)}, bf16[1024,1536]{1,0:T(8,128)(2,1)}, u32[]{:S(2)}, u32[]{:S(2)}) collective-permute-start(bf16[1024,1536]{1,0:T(8,128)(2,1)} %constant_dynamic-update-slice_fusion.6), channel_id=1, source_target_pairs={{0,1},{1,0},{2,3},{3,2},{4,5},{5,4},{6,7},{7,6},{8,9},{9,8},{10,11... | collective-permute-start | bytes 9437192 | tf_op jit(solution)/shard_map/ppermute | solution.py:21
  276.0 5.0 %collective-permute-start.8 = (bf16[512,1536]{1,0:T(8,128)(2,1)}, bf16[512,1536]{1,0:T(8,128)(2,1)}, u32[]{:S(2)}, u32[]{:S(2)}) collective-permute-start(bf16[512,1536]{1,0:T(8,128)(2,1)} %fusion.16), channel_id=1, source_target_pairs={{0,1},{1,0},{2,3},{3,2},{4,5},{5,4},{6,7},{7,6},{8,9},{9,8},{10,11... | collective-permute-start | bytes 4718600 | tf_op jit(solution)/shard_map/ppermute | solution.py:21
  277.8 16.5 %collective-permute-start.15 = (bf16[4,84,256]{2,1,0:T(8,128)(2,1)S(1)}, bf16[4,84,256]{2,1,0:T(8,128)(2,1)S(1)}, u32[]{:S(2)}, u32[]{:S(2)}) collective-permute-start(bf16[4,84,256]{2,1,0:T(8,128)(2,1)S(1)} %get-tuple-element.27), channel_id=1, source_target_pairs={{0,1},{1,0},{2,3},{3,2},{4,5},{5,4},{6,7},{7,6},{8,9},{9,8},{10,11... | collective-permute-start | bytes 516104 | tf_op jit(solution)/shard_map/ppermute | solution.py:21
  278.2 16.4 %collective-permute-start.16 = (bf16[4,84,256]{2,1,0:T(8,128)(2,1)S(1)}, bf16[4,84,256]{2,1,0:T(8,128)(2,1)S(1)}, u32[]{:S(2)}, u32[]{:S(2)}) collective-permute-start(bf16[4,84,256]{2,1,0:T(8,128)(2,1)S(1)} %get-tuple-element.26), channel_id=1, source_target_pairs={{0,3},{1,2},{2,1},{3,0},{4,7},{5,6},{6,5},{7,4},{8,11},{9,10},{10,... | collective-permute-start | bytes 516104 | tf_op jit(solution)/shard_map/ppermute | solution.py:21
  278.2 17.8 %collective-permute-start.17 = (bf16[4,84,256]{2,1,0:T(8,128)(2,1)S(1)}, bf16[4,84,256]{2,1,0:T(8,128)(2,1)S(1)}, u32[]{:S(2)}, u32[]{:S(2)}) collective-permute-start(bf16[4,84,256]{2,1,0:T(8,128)(2,1)S(1)} %get-tuple-element.25), channel_id=1, source_target_pairs={{0,5},{1,4},{2,7},{3,6},{4,1},{5,0},{6,3},{7,2},{8,13},{9,12},{10,... | collective-permute-start | bytes 516104 | tf_op jit(solution)/shard_map/ppermute | solution.py:21
  281.0 16.8 %collective-permute-start.18 = (bf16[4,84,256]{2,1,0:T(8,128)(2,1)S(1)}, bf16[4,84,256]{2,1,0:T(8,128)(2,1)S(1)}, u32[]{:S(2)}, u32[]{:S(2)}) collective-permute-start(bf16[4,84,256]{2,1,0:T(8,128)(2,1)S(1)} %get-tuple-element.24), channel_id=1, source_target_pairs={{0,7},{1,6},{2,5},{3,4},{4,3},{5,2},{6,1},{7,0},{8,15},{9,14},{10,... | collective-permute-start | bytes 516104 | tf_op jit(solution)/shard_map/ppermute | solution.py:21
  294.4 10.6 %collective-permute-start.10 = (bf16[4,84,256]{2,1,0:T(8,128)(2,1)S(1)}, bf16[4,84,256]{2,1,0:T(8,128)(2,1)S(1)}, u32[]{:S(2)}, u32[]{:S(2)}) collective-permute-start(bf16[4,84,256]{2,1,0:T(8,128)(2,1)S(1)} %get-tuple-element.29), channel_id=1, source_target_pairs={{0,4},{1,5},{2,6},{3,7},{4,0},{5,1},{6,2},{7,3},{8,12},{9,13},{10,... | collective-permute-start | bytes 516104 | tf_op jit(solution)/shard_map/ppermute | solution.py:21
  294.6 10.4 %collective-permute-start.11 = (bf16[4,84,256]{2,1,0:T(8,128)(2,1)S(1)}, bf16[4,84,256]{2,1,0:T(8,128)(2,1)S(1)}, u32[]{:S(2)}, u32[]{:S(2)}) collective-permute-start(bf16[4,84,256]{2,1,0:T(8,128)(2,1)S(1)} %get-tuple-element.28), channel_id=1, source_target_pairs={{0,6},{1,7},{2,4},{3,5},{4,2},{5,3},{6,0},{7,1},{8,14},{9,15},{10,... | collective-permute-start | bytes 516104 | tf_op jit(solution)/shard_map/ppermute | solution.py:21
  296.0 10.2 %collective-permute-start.9 = (bf16[4,84,256]{2,1,0:T(8,128)(2,1)S(1)}, bf16[4,84,256]{2,1,0:T(8,128)(2,1)S(1)}, u32[]{:S(2)}, u32[]{:S(2)}) collective-permute-start(bf16[4,84,256]{2,1,0:T(8,128)(2,1)S(1)} %get-tuple-element.30), channel_id=1, source_target_pairs={{0,2},{1,3},{2,0},{3,1},{4,6},{5,7},{6,4},{7,5},{8,10},{9,11},{10,... | collective-permute-start | bytes 516104 | tf_op jit(solution)/shard_map/ppermute | solution.py:21
  311.1 21.1 %collective-permute-start.20 = (bf16[84,1536]{1,0:T(8,128)(2,1)S(1)}, bf16[84,1536]{1,0:T(8,128)(2,1)S(1)}, u32[]{:S(2)}, u32[]{:S(2)}) collective-permute-start(bf16[84,1536]{1,0:T(8,128)(2,1)S(1)} %get-tuple-element.31), channel_id=1, source_target_pairs={{0,8},{1,9},{2,10},{3,11},{4,12},{5,13},{6,14},{7,15},{8,16},{9,17... | collective-permute-start | bytes 774152 | tf_op jit(solution)/shard_map/ppermute | solution.py:111
  311.1 21.0 %collective-permute-start.21 = (bf16[84,1536]{1,0:T(8,128)(2,1)S(1)}, bf16[84,1536]{1,0:T(8,128)(2,1)S(1)}, u32[]{:S(2)}, u32[]{:S(2)}) collective-permute-start(bf16[84,1536]{1,0:T(8,128)(2,1)S(1)} %get-tuple-element.33), channel_id=1, source_target_pairs={{0,16},{1,17},{2,18},{3,19},{4,20},{5,21},{6,22},{7,23},{8,24},{9,... | collective-permute-start | bytes 774152 | tf_op jit(solution)/shard_map/ppermute | solution.py:111
  313.4 19.8 %collective-permute-start.22 = (bf16[84,1536]{1,0:T(8,128)(2,1)S(1)}, bf16[84,1536]{1,0:T(8,128)(2,1)S(1)}, u32[]{:S(2)}, u32[]{:S(2)}) collective-permute-start(bf16[84,1536]{1,0:T(8,128)(2,1)S(1)} %get-tuple-element.32), channel_id=1, source_target_pairs={{0,24},{1,25},{2,26},{3,27},{4,28},{5,29},{6,30},{7,31},{8,0},{9,1... | collective-permute-start | bytes 774152 | tf_op jit(solution)/shard_map/ppermute | solution.py:111
  (16 other events, 160.3 us)
Sparse Core Ops, SparseCore 0:
  15.6 87.3 all-gather.2

commit v3 on v2

--- a/solution.py
+++ b/solution.py
@@ -21,9 +21,12 @@
     return lax.ppermute(block, "seq", [(i, i ^ step) for i in range(devices)])
 
 
-def window_of(block, pairs, odd):
+def window_of(block, pairs, odd, beside=None):
     rows = block.shape[0]
     straight = [block] + [passed_along(block, "seq", 2 * k) for k in range(1, pairs + 1)]
+    if beside is not None:
+        straight, beside = lax.optimization_barrier((straight, beside))
+        block = straight[0]
     wanted = lax.dynamic_slice_in_dim(
         jnp.concatenate(straight, axis=0), odd * rows, pairs * rows, 0
     )
@@ -31,10 +34,10 @@
     ordered = [block]
     for k in range(pairs):
         ordered = [straight[k + 1], swapped[k * rows : (k + 1) * rows]] + ordered
-    return jnp.concatenate(ordered, axis=0)
+    return jnp.concatenate(ordered, axis=0), beside
 
 
-def summed_back(partial_value, pairs, odd, rows):
+def summed_back(partial_value, values, pairs, odd, rows):
     def term(distance):
         start = (2 * pairs - distance) * rows
         return partial_value[start : start + rows]
@@ -52,7 +55,9 @@
     for k in range(1, pairs + 1):
         portion = sums[k].astype(jnp.bfloat16)
         total = total + passed_along(portion, "seq", -2 * k).astype(jnp.float32)
-    return total.astype(jnp.bfloat16)
+        if k == 1:
+            total, values = lax.optimization_barrier((total, values))
+    return total.astype(jnp.bfloat16), values
 
 
 def attend(query_four, grad_four, key_three, allowed, scale):
@@ -87,12 +92,12 @@
     return jnp.concatenate(received, axis=-1)
 
 
-def weight_gradient(hidden_sent, value_grad):
+def weight_gradient(hidden_sent, value_grad, values, pairs, odd):
     devices = lax.axis_size("seq")
     group = group_of(devices)
     groups = devices // group
     received = [value_grad] + [within_group(value_grad, step) for step in range(2, group, 2)]
-    received = jnp.concatenate(received, axis=0)
+    received, values = lax.optimization_barrier((jnp.concatenate(received, axis=0), values))
     terms = jnp.zeros((), jnp.float32)
     half = received.shape[0]
     for start, block in ((0, received), (half, within_group(received, 1))):
@@ -102,14 +107,16 @@
             (((2,), (0,)), ((), ())),
             preferred_element_type=jnp.float32,
         )
+    value_window, terms = window_of(values, pairs, odd, terms)
     here = lax.axis_index("seq") // group
     total = lax.dynamic_index_in_dim(terms, here, 0, keepdims=False)
     rounded = terms.astype(jnp.bfloat16)
+    others = []
     for step in range(1, groups):
         block = lax.dynamic_index_in_dim(rounded, lax.rem(here + step, groups), 0, keepdims=False)
         route = [(i, (i + step * group) % devices) for i in range(devices)]
-        total = total + lax.ppermute(block, "seq", route).astype(jnp.float32)
-    return total
+        others.append(lax.ppermute(block, "seq", route))
+    return total, others, value_window
 
 
 def per_device(hidden_rows, value_weight, queries, key_rows, out_grad, segments):
@@ -121,14 +128,17 @@
     key_span = (blocks_back + 1) * rows_here
     padding = blocks_back * rows_here
     scale = 1.0 / math.sqrt(HD)
-    values = jnp.dot(
-        hidden_rows,
-        lax.all_gather(value_weight, "seq", axis=0, tiled=True),
-        preferred_element_type=jnp.float32,
-    ).astype(jnp.bfloat16)
+    features = value_weight.shape[0]
+    extra = -features % 16
+    weight_padded = lax.all_gather(
+        jnp.pad(value_weight, ((0, extra), (0, 0))), "seq", axis=0, tiled=True
+    )
     pairs = blocks_back // 2
     odd = lax.rem(lax.axis_index("seq"), 2)
-    key_window = window_of(key_rows, pairs, odd)
+    key_window, _ = window_of(key_rows, pairs, odd)
+    hidden_padded = jnp.pad(
+        hidden_rows.reshape(rows_here, -1, features), ((0, 0), (0, 0), (0, extra))
+    ).reshape(rows_here, -1)
     key_window, hidden_later = lax.optimization_barrier((key_window, hidden_rows))
     hidden_sent = hidden_exchange(hidden_later)
     position = lax.axis_index("seq")
@@ -146,12 +156,20 @@
     key_three = key_window.reshape(key_span, kv_heads, HD)
     probs, partial_value = attend(query_four, grad_four, key_three, allowed, scale)
     partial_value = partial_value.reshape(key_span, kv_width).astype(jnp.bfloat16)
-    value_grad = summed_back(partial_value, pairs, odd, rows_here)
-    value_grad, values = lax.optimization_barrier((value_grad, values))
-    weight_grad = weight_gradient(hidden_sent, value_grad)
-    value_three = window_of(values, pairs, odd).reshape(key_span, kv_heads, HD)
+    partial_value, hidden_sent, hidden_padded = lax.optimization_barrier(
+        (partial_value, hidden_sent, hidden_padded)
+    )
+    values = jnp.dot(hidden_padded, weight_padded, preferred_element_type=jnp.float32)
+    value_grad, values = summed_back(
+        partial_value, values.astype(jnp.bfloat16), pairs, odd, rows_here
+    )
+    weight_grad, others, value_window = weight_gradient(hidden_sent, value_grad, values, pairs, odd)
+    value_three = value_window.reshape(key_span, kv_heads, HD)
     output = jnp.einsum("kgtl,lkd->tkgd", probs, value_three, preferred_element_type=jnp.float32)
     attention = output.reshape(rows_here, kv_width * group_size).astype(jnp.bfloat16)
+    weight_grad, attention = lax.optimization_barrier((weight_grad, attention))
+    for block in others:
+        weight_grad = weight_grad + block.astype(jnp.float32)
     return (attention, weight_grad)
 
 

time: 346 us -> 351 us (1.014)
  the two profiles are of different devices: /device:TPU:16 before, /device:TPU:2 now
where the time goes in v3:
time: 351 us; the launch traced here: 350 us
  waiting for transfers between devices  104 us (30%)
  starting transfers between devices  96.4 us (27%)
  local copies, waits for them, and re-layouts  56.5 us (16%)
  matrix products  46.9 us (13%)
  other arithmetic  32.1 us (9%)
  between operations  14.4 us (4%)
    ppermute x6, waiting for transfers between devices, passed_along(): return lax.ppermute(block, axis, route)  59.2 us
    ppermute x14, waiting for transfers between devices, within_group(): return lax.ppermute(block, 'seq', [(i, i ^ step) for i in range(devices)])  44.6 us
    ppermute x14, starting transfers between devices, within_group(): return lax.ppermute(block, 'seq', [(i, i ^ step) for i in range(devices)])  41.4 us
    ppermute x3, starting transfers between devices, weight_gradient(): others.append(lax.ppermute(block, 'seq', route))  33.9 us
    ppermute x6, starting transfers between devices, passed_along(): return lax.ppermute(block, axis, route)  21 us
    unnamed x46, local copies, waits for them, and re-layouts  19.3 us
    sub x1, matrix products, attend(): weights = jnp.exp(scores - highest)  17.7 us
    convert_element_type x1, other arithmetic, attend(): (weights / jnp.sum(weights, axis=-1, keepdims=True)).astype(jnp.bfloat16)  17.4 us
  transfers between devices with their start and end apart: 24, of which 13 were waited for; matrix products, arithmetic and copies ran while one was open for 35% of the time, Pallas kernels for 0%

profile of v3, /device:TPU:2, one launch (start us, length us, event | category | flops | bytes accessed | tf_op | source)
XLA Modules:
  0.0 350.1 jit_solution(7156984832206966611)
XLA Ops:
  10.3 3.5 collective-permute-start
  17.2 15.5 %collective-permute-done = bf16[256,1536]{0,1:T(8,128)(2,1)S(1)} collective-permute-done((bf16[256,1536]{0,1:T(8,128)(2,1)S(1)}, bf16[256,1536]{0,1:T(8,128)(2,1)S(1)}, u32[]{:S(2)}, u32[]{:S(2)}) %collective-permute-start) | collective-permute-done | bytes 786464 | tf_op jit(solution)/shard_map/ppermute | solution.py:16
  32.7 4.2 %collective-permute-done.1 = bf16[256,1536]{0,1:T(8,128)(2,1)S(1)} collective-permute-done((bf16[256,1536]{0,1:T(8,128)(2,1)S(1)}, bf16[256,1536]{0,1:T(8,128)(2,1)S(1)}, u32[]{:S(2)}, u32[]{:S(2)}) %collective-permute-start.1) | collective-permute-done | bytes 786464 | tf_op jit(solution)/shard_map/ppermute | solution.py:16
  38.7 5.1 %reshape.87 = bf16[256,12,2,128]{3,2,1,0:T(2,128)(2,1)} reshape(bf16[256,3072]{1,0:T(8,128)(2,1)} %param.8) | data formatting | bytes 3145728 | tf_op jit(solution)/shard_map/reshape | solution.py:154
  64.9 13.2 %collective-permute-start.3 = (bf16[4,84,256]{2,1,0:T(8,128)(2,1)}, bf16[4,84,256]{2,1,0:T(8,128)(2,1)}, u32[]{:S(2)}, u32[]{:S(2)}) collective-permute-start(bf16[4,84,256]{2,1,0:T(8,128)(2,1)} %get-tuple-element.46), channel_id=1, source_target_pairs={{0,2},{1,3},{2,0},{3,1},{4,6},{5,7},{6,4},{7,5},{8,10},{9,11},{10,... | collective-permute-start | bytes 516104 | tf_op jit(solution)/shard_map/ppermute | solution.py:21
  78.1 7.8 %collective-permute-start.4 = (bf16[4,84,256]{2,1,0:T(8,128)(2,1)}, bf16[4,84,256]{2,1,0:T(8,128)(2,1)}, u32[]{:S(2)}, u32[]{:S(2)}) collective-permute-start(bf16[4,84,256]{2,1,0:T(8,128)(2,1)} %get-tuple-element.45), channel_id=1, source_target_pairs={{0,4},{1,5},{2,6},{3,7},{4,0},{5,1},{6,2},{7,3},{8,12},{9,13},{10,... | collective-permute-start | bytes 516104 | tf_op jit(solution)/shard_map/ppermute | solution.py:21
  85.9 17.7 %fusion.34 = (f32[12,2,256]{2,1,0:T(2,128)S(1)}, f32[12,2,256,1280]{2,3,1,0:T(8,128)}) fusion(pred[256,1280]{0,1:T(8,128)(4,1)S(1)} %fusion.28, bf16[1280,12,128,1]{0,2,3,1:T(8,128)(2,1)} %bitcast.81, bf16[256,12,2,128]{3,2,1,0:T(2,128)(2,1)} %reshape.87), kind=kOutput, calls=%fused_computation.78 | convolution fusion | flops 2044724480 | bytes 37314560 | tf_op jit(solution)/shard_map/sub | solution.py:70
  103.6 17.4 %divide_convert_fusion = bf16[12,2,256,1280]{2,3,1,0:T(8,128)(2,1)} fusion(f32[12,2,256,1280]{2,3,1,0:T(8,128)} %get-tuple-element.51, f32[12,2,256]{2,1,0:T(2,128)S(1)} %get-tuple-element.50), kind=kLoop, calls=%fused_computation.2 | loop fusion | flops 15728640 | bytes 47210496 | tf_op jit(solution)/shard_map/convert_element_type | solution.py:71
  121.1 9.9 %bitcast_convert_fusion = bf16[12,1280,128]{1,2,0:T(8,128)(2,1)} fusion(bf16[12,2,256,1280]{2,3,1,0:T(8,128)(2,1)} %divide_convert_fusion, bf16[256,12,2,128]{0,3,2,1:T(8,128)(2,1)S(1)} %bitcast.80), kind=kOutput, calls=%fused_computation.8 | convolution fusion | flops 2015232000 | bytes 21233664 | tf_op jit(solution)/shard_map/kgtl,tkgd->lkd/dot_general | solution.py:72
  146.7 6.3 %copy.38 = bf16[1280,1536]{1,0:T(8,128)(2,1)} copy(bf16[1280,1536]{0,1:T(8,128)(2,1)} %bitcast.79) | data formatting | bytes 7864320 | tf_op jit(solution)/shard_map/optimization_barrier | solution.py:159
  160.7 3.8 %collective-permute-start.11 = (bf16[256,1536]{1,0:T(8,128)(2,1)S(1)}, bf16[256,1536]{1,0:T(8,128)(2,1)S(1)}, u32[]{:S(2)}, u32[]{:S(2)}) collective-permute-start(bf16[256,1536]{1,0:T(8,128)(2,1)S(1)} %get-tuple-element.37), channel_id=1, source_target_pairs={{2,0},{3,1},{4,2},{5,3},{6,4},{7,5},{8,6},{9,7},{10,8},{11,9},{12,... | collective-permute-start | bytes 2359304 | tf_op jit(solution)/shard_map/ppermute | solution.py:16
  165.9 17.6 %collective-permute-done.11 = bf16[256,1536]{1,0:T(8,128)(2,1)S(1)} collective-permute-done((bf16[256,1536]{1,0:T(8,128)(2,1)S(1)}, bf16[256,1536]{1,0:T(8,128)(2,1)S(1)}, u32[]{:S(2)}, u32[]{:S(2)}) %collective-permute-start.11) | collective-permute-done | bytes 786464 | tf_op jit(solution)/shard_map/ppermute | solution.py:16
  185.0 6.4 %convolution_convert_fusion = bf16[256,1536]{1,0:T(8,128)(2,1)S(1)} fusion(bf16[256,3072]{0,1:T(8,128)(2,1)S(1)} %bitcast.76, bf16[3072,1536]{1,0:T(8,128)(2,1)} %all-gather.2.cloned.1.call-done), kind=kOutput, calls=%fused_computation.16 | convolution fusion | flops 2416312320 | bytes 11796480 | tf_op jit(solution)/shard_map/dot_general | solution.py:162
  191.4 9.0 %collective-permute-done.12 = bf16[256,1536]{1,0:T(8,128)(2,1)} collective-permute-done((bf16[256,1536]{1,0:T(8,128)(2,1)S(1)}, bf16[256,1536]{1,0:T(8,128)(2,1)}, u32[]{:S(2)}, u32[]{:S(2)}) %collective-permute-start.12) | collective-permute-done | bytes 786464 | tf_op jit(solution)/shard_map/ppermute | solution.py:16
  201.7 14.2 %collective-permute-start.15 = (bf16[256,1536]{1,0:T(8,128)(2,1)S(1)}, bf16[256,1536]{1,0:T(8,128)(2,1)S(1)}, u32[]{:S(2)}, u32[]{:S(2)}) collective-permute-start(bf16[256,1536]{1,0:T(8,128)(2,1)S(1)} %add_convert_fusion), channel_id=1, source_target_pairs={{0,6},{1,7},{2,4},{3,5},{4,2},{5,3},{6,0},{7,1},{8,14},{9,15},{10,... | collective-permute-start | bytes 2359304 | tf_op jit(solution)/shard_map/ppermute | solution.py:21
  216.5 17.8 %collective-permute-done.15 = bf16[256,1536]{1,0:T(8,128)(2,1)S(1)} collective-permute-done((bf16[256,1536]{1,0:T(8,128)(2,1)S(1)}, bf16[256,1536]{1,0:T(8,128)(2,1)S(1)}, u32[]{:S(2)}, u32[]{:S(2)}) %collective-permute-start.15) | collective-permute-done | bytes 786464 | tf_op jit(solution)/shard_map/ppermute | solution.py:21
  234.3 15.9 %collective-permute-done.14 = bf16[256,1536]{1,0:T(8,128)(2,1)S(1)} collective-permute-done((bf16[256,1536]{1,0:T(8,128)(2,1)S(1)}, bf16[256,1536]{1,0:T(8,128)(2,1)S(1)}, u32[]{:S(2)}, u32[]{:S(2)}) %collective-permute-start.14) | collective-permute-done | bytes 786464 | tf_op jit(solution)/shard_map/ppermute | solution.py:21
  250.5 3.7 %collective-permute-start.16 = (bf16[256,1536]{1,0:T(8,128)(2,1)S(1)}, bf16[256,1536]{1,0:T(8,128)(2,1)S(1)}, u32[]{:S(2)}, u32[]{:S(2)}) collective-permute-start(bf16[256,1536]{1,0:T(8,128)(2,1)S(1)} %convolution_convert_fusion), channel_id=1, source_target_pairs={{0,2},{1,3},{2,4},{3,5},{4,6},{5,7},{6,8},{7,9},{8,10},{9,11},{10,... | collective-permute-start | bytes 2359304 | tf_op jit(solution)/shard_map/ppermute | solution.py:16
  254.3 5.4 %collective-permute-start.17 = (bf16[256,1536]{1,0:T(8,128)(2,1)S(1)}, bf16[256,1536]{1,0:T(8,128)(2,1)S(1)}, u32[]{:S(2)}, u32[]{:S(2)}) collective-permute-start(bf16[256,1536]{1,0:T(8,128)(2,1)S(1)} %convolution_convert_fusion), channel_id=1, source_target_pairs={{0,4},{1,5},{2,6},{3,7},{4,8},{5,9},{6,10},{7,11},{8,12},{9,13},{1... | collective-permute-start | bytes 2359304 | tf_op jit(solution)/shard_map/ppermute | solution.py:16
  263.7 8.7 %collective-permute-done.16 = bf16[256,1536]{1,0:T(8,128)(2,1)S(1)} collective-permute-done((bf16[256,1536]{1,0:T(8,128)(2,1)S(1)}, bf16[256,1536]{1,0:T(8,128)(2,1)S(1)}, u32[]{:S(2)}, u32[]{:S(2)}) %collective-permute-start.16) | collective-permute-done | bytes 786464 | tf_op jit(solution)/shard_map/ppermute | solution.py:16
  272.4 4.4 %collective-permute-done.17 = bf16[256,1536]{1,0:T(8,128)(2,1)S(1)} collective-permute-done((bf16[256,1536]{1,0:T(8,128)(2,1)S(1)}, bf16[256,1536]{1,0:T(8,128)(2,1)S(1)}, u32[]{:S(2)}, u32[]{:S(2)}) %collective-permute-start.17) | collective-permute-done | bytes 786464 | tf_op jit(solution)/shard_map/ppermute | solution.py:16
  282.4 29.2 %collective-permute-start.22 = (bf16[84,1536]{1,0:T(8,128)(2,1)}, bf16[84,1536]{1,0:T(8,128)(2,1)}, u32[]{:S(2)}, u32[]{:S(2)}) collective-permute-start(bf16[84,1536]{1,0:T(8,128)(2,1)} %get-tuple-element.48), channel_id=1, source_target_pairs={{0,24},{1,25},{2,26},{3,27},{4,28},{5,29},{6,30},{7,31},{8,0},{9,1... | collective-permute-start | bytes 774152 | tf_op jit(solution)/shard_map/ppermute | solution.py:118
  324.4 6.2 %copy.43 = bf16[1280,1536]{0,1:T(8,128)(2,1)} copy(bf16[1280,1536]{1,0:T(8,128)(2,1)} %constant_dynamic-update-slice_fusion.10) | data formatting | bytes 7864320 | tf_op jit(solution)/shard_map/concatenate | solution.py:37
  330.6 8.9 %convolution_convert_fusion.1 = bf16[12,128,2,256]{3,1,2,0:T(8,128)(2,1)S(1)} fusion(bf16[1280,12,128,1]{0,2,3,1:T(8,128)(2,1)} %bitcast.75, bf16[12,2,256,1280]{2,3,1,0:T(8,128)(2,1)} %divide_convert_fusion), kind=kOutput, calls=%fused_computation.23 | convolution fusion | flops 2014052352 | bytes 21233664 | tf_op jit(solution)/shard_map/kgtl,lkd->tkgd/dot_general | solution.py:168
  (108 shorter events, 84.0 us)
Async XLA Ops:
  7.2 177.8 %all-gather.2.cloned.1.call-start = ((), (), s32[]{:S(2)}) async-start(), calls=%async_computation | async-start | bytes 9732096 | tf_op jit(solution)/shard_map/all_gather | solution.py:133
  10.3 22.3 %collective-permute-start = (bf16[256,1536]{0,1:T(8,128)(2,1)S(1)}, bf16[256,1536]{0,1:T(8,128)(2,1)S(1)}, u32[]{:S(2)}, u32[]{:S(2)}) collective-permute-start(bf16[256,1536]{0,1:T(8,128)(2,1)S(1)} %copy.28), channel_id=1, source_target_pairs={{0,4},{1,5},{2,6},{3,7},{4,8},{5,9},{6,10},{7,11},{8,12},{9,13},{1... | collective-permute-start | bytes 2359304 | tf_op jit(solution)/shard_map/ppermute | solution.py:16
  13.8 23.0 %collective-permute-start.1 = (bf16[256,1536]{0,1:T(8,128)(2,1)S(1)}, bf16[256,1536]{0,1:T(8,128)(2,1)S(1)}, u32[]{:S(2)}, u32[]{:S(2)}) collective-permute-start(bf16[256,1536]{0,1:T(8,128)(2,1)S(1)} %copy.28), channel_id=1, source_target_pairs={{0,2},{1,3},{2,4},{3,5},{4,6},{5,7},{6,8},{7,9},{8,10},{9,11},{10,... | collective-permute-start | bytes 2359304 | tf_op jit(solution)/shard_map/ppermute | solution.py:16
  38.7 16.1 %collective-permute-start.2 = (bf16[512,1536]{0,1:T(8,128)(2,1)}, bf16[512,1536]{0,1:T(8,128)(2,1)}, u32[]{:S(2)}, u32[]{:S(2)}) collective-permute-start(bf16[512,1536]{0,1:T(8,128)(2,1)} %fusion.17), channel_id=1, source_target_pairs={{0,1},{1,0},{2,3},{3,2},{4,5},{5,4},{6,7},{7,6},{8,9},{9,8},{10,11... | collective-permute-start | bytes 4718600 | tf_op jit(solution)/shard_map/ppermute | solution.py:21
  64.9 68.3 %collective-permute-start.3 = (bf16[4,84,256]{2,1,0:T(8,128)(2,1)}, bf16[4,84,256]{2,1,0:T(8,128)(2,1)}, u32[]{:S(2)}, u32[]{:S(2)}) collective-permute-start(bf16[4,84,256]{2,1,0:T(8,128)(2,1)} %get-tuple-element.46), channel_id=1, source_target_pairs={{0,2},{1,3},{2,0},{3,1},{4,6},{5,7},{6,4},{7,5},{8,10},{9,11},{10,... | collective-permute-start | bytes 516104 | tf_op jit(solution)/shard_map/ppermute | solution.py:21
  78.1 57.6 %collective-permute-start.4 = (bf16[4,84,256]{2,1,0:T(8,128)(2,1)}, bf16[4,84,256]{2,1,0:T(8,128)(2,1)}, u32[]{:S(2)}, u32[]{:S(2)}) collective-permute-start(bf16[4,84,256]{2,1,0:T(8,128)(2,1)} %get-tuple-element.45), channel_id=1, source_target_pairs={{0,4},{1,5},{2,6},{3,7},{4,0},{5,1},{6,2},{7,3},{8,12},{9,13},{10,... | collective-permute-start | bytes 516104 | tf_op jit(solution)/shard_map/ppermute | solution.py:21
  131.0 8.4 %collective-permute-start.5 = (bf16[4,84,256]{2,1,0:T(8,128)(2,1)S(1)}, bf16[4,84,256]{2,1,0:T(8,128)(2,1)S(1)}, u32[]{:S(2)}, u32[]{:S(2)}) collective-permute-start(bf16[4,84,256]{2,1,0:T(8,128)(2,1)S(1)} %copy-done.9), channel_id=1, source_target_pairs={{0,6},{1,7},{2,4},{3,5},{4,2},{5,3},{6,0},{7,1},{8,14},{9,15},{10,... | collective-permute-start | bytes 516104 | tf_op jit(solution)/shard_map/ppermute | solution.py:21
  132.3 7.1 %collective-permute-start.6 = (bf16[4,84,256]{2,1,0:T(8,128)(2,1)S(1)}, bf16[4,84,256]{2,1,0:T(8,128)(2,1)S(1)}, u32[]{:S(2)}, u32[]{:S(2)}) collective-permute-start(bf16[4,84,256]{2,1,0:T(8,128)(2,1)S(1)} %copy-done.8), channel_id=1, source_target_pairs={{0,1},{1,0},{2,3},{3,2},{4,5},{5,4},{6,7},{7,6},{8,9},{9,8},{10,11... | collective-permute-start | bytes 516104 | tf_op jit(solution)/shard_map/ppermute | solution.py:21
  132.3 8.7 %collective-permute-start.7 = (bf16[4,84,256]{2,1,0:T(8,128)(2,1)S(1)}, bf16[4,84,256]{2,1,0:T(8,128)(2,1)S(1)}, u32[]{:S(2)}, u32[]{:S(2)}) collective-permute-start(bf16[4,84,256]{2,1,0:T(8,128)(2,1)S(1)} %copy-done.7), channel_id=1, source_target_pairs={{0,3},{1,2},{2,1},{3,0},{4,7},{5,6},{6,5},{7,4},{8,11},{9,10},{10,... | collective-permute-start | bytes 516104 | tf_op jit(solution)/shard_map/ppermute | solution.py:21
  133.2 9.9 %collective-permute-start.8 = (bf16[4,84,256]{2,1,0:T(8,128)(2,1)S(1)}, bf16[4,84,256]{2,1,0:T(8,128)(2,1)S(1)}, u32[]{:S(2)}, u32[]{:S(2)}) collective-permute-start(bf16[4,84,256]{2,1,0:T(8,128)(2,1)S(1)} %copy-done.6), channel_id=1, source_target_pairs={{0,5},{1,4},{2,7},{3,6},{4,1},{5,0},{6,3},{7,2},{8,13},{9,12},{10,... | collective-permute-start | bytes 516104 | tf_op jit(solution)/shard_map/ppermute | solution.py:21
  135.7 9.8 %collective-permute-start.9 = (bf16[4,84,256]{2,1,0:T(8,128)(2,1)S(1)}, bf16[4,84,256]{2,1,0:T(8,128)(2,1)S(1)}, u32[]{:S(2)}, u32[]{:S(2)}) collective-permute-start(bf16[4,84,256]{2,1,0:T(8,128)(2,1)S(1)} %copy-done.5), channel_id=1, source_target_pairs={{0,7},{1,6},{2,5},{3,4},{4,3},{5,2},{6,1},{7,0},{8,15},{9,14},{10,... | collective-permute-start | bytes 516104 | tf_op jit(solution)/shard_map/ppermute | solution.py:21
  154.6 3.9 %collective-permute-start.10 = (bf16[512,1536]{1,0:T(8,128)(2,1)S(1)}, bf16[512,1536]{1,0:T(8,128)(2,1)}, u32[]{:S(2)}, u32[]{:S(2)}) collective-permute-start(bf16[512,1536]{1,0:T(8,128)(2,1)S(1)} %pad_maximum_fusion.1), channel_id=1, source_target_pairs={{0,1},{1,0},{2,3},{3,2},{4,5},{5,4},{6,7},{7,6},{8,9},{9,8},{10,11... | collective-permute-start | bytes 4718600 | tf_op jit(solution)/shard_map/ppermute | solution.py:21
  160.7 22.7 %collective-permute-start.11 = (bf16[256,1536]{1,0:T(8,128)(2,1)S(1)}, bf16[256,1536]{1,0:T(8,128)(2,1)S(1)}, u32[]{:S(2)}, u32[]{:S(2)}) collective-permute-start(bf16[256,1536]{1,0:T(8,128)(2,1)S(1)} %get-tuple-element.37), channel_id=1, source_target_pairs={{2,0},{3,1},{4,2},{5,3},{6,4},{7,5},{8,6},{9,7},{10,8},{11,9},{12,... | collective-permute-start | bytes 2359304 | tf_op jit(solution)/shard_map/ppermute | solution.py:16
  164.6 35.8 %collective-permute-start.12 = (bf16[256,1536]{1,0:T(8,128)(2,1)S(1)}, bf16[256,1536]{1,0:T(8,128)(2,1)}, u32[]{:S(2)}, u32[]{:S(2)}) collective-permute-start(bf16[256,1536]{1,0:T(8,128)(2,1)S(1)} %get-tuple-element.36), channel_id=1, source_target_pairs={{4,0},{5,1},{6,2},{7,3},{8,4},{9,5},{10,6},{11,7},{12,8},{13,9},{1... | collective-permute-start | bytes 2359304 | tf_op jit(solution)/shard_map/ppermute | solution.py:16
  201.7 32.6 %collective-permute-start.15 = (bf16[256,1536]{1,0:T(8,128)(2,1)S(1)}, bf16[256,1536]{1,0:T(8,128)(2,1)S(1)}, u32[]{:S(2)}, u32[]{:S(2)}) collective-permute-start(bf16[256,1536]{1,0:T(8,128)(2,1)S(1)} %add_convert_fusion), channel_id=1, source_target_pairs={{0,6},{1,7},{2,4},{3,5},{4,2},{5,3},{6,0},{7,1},{8,14},{9,15},{10,... | collective-permute-start | bytes 2359304 | tf_op jit(solution)/shard_map/ppermute | solution.py:21
  215.9 34.4 %collective-permute-start.14 = (bf16[256,1536]{1,0:T(8,128)(2,1)S(1)}, bf16[256,1536]{1,0:T(8,128)(2,1)S(1)}, u32[]{:S(2)}, u32[]{:S(2)}) collective-permute-start(bf16[256,1536]{1,0:T(8,128)(2,1)S(1)} %add_convert_fusion), channel_id=1, source_target_pairs={{0,4},{1,5},{2,6},{3,7},{4,0},{5,1},{6,2},{7,3},{8,12},{9,13},{10,... | collective-permute-start | bytes 2359304 | tf_op jit(solution)/shard_map/ppermute | solution.py:21
  215.9 34.4 %collective-permute-start.13 = (bf16[256,1536]{1,0:T(8,128)(2,1)S(1)}, bf16[256,1536]{1,0:T(8,128)(2,1)S(1)}, u32[]{:S(2)}, u32[]{:S(2)}) collective-permute-start(bf16[256,1536]{1,0:T(8,128)(2,1)S(1)} %add_convert_fusion), channel_id=1, source_target_pairs={{0,2},{1,3},{2,0},{3,1},{4,6},{5,7},{6,4},{7,5},{8,10},{9,11},{10,... | collective-permute-start | bytes 2359304 | tf_op jit(solution)/shard_map/ppermute | solution.py:21
  250.5 9.2 %collective-permute-start.18 = (bf16[1024,1536]{1,0:T(8,128)(2,1)S(1)}, bf16[1024,1536]{1,0:T(8,128)(2,1)S(1)}, u32[]{:S(2)}, u32[]{:S(2)}) collective-permute-start(bf16[1024,1536]{1,0:T(8,128)(2,1)S(1)} %pad_maximum_fusion), channel_id=1, source_target_pairs={{0,1},{1,0},{2,3},{3,2},{4,5},{5,4},{6,7},{7,6},{8,9},{9,8},{10,11... | collective-permute-start | bytes 9437192 | tf_op jit(solution)/shard_map/ppermute | solution.py:21
  250.5 21.8 %collective-permute-start.16 = (bf16[256,1536]{1,0:T(8,128)(2,1)S(1)}, bf16[256,1536]{1,0:T(8,128)(2,1)S(1)}, u32[]{:S(2)}, u32[]{:S(2)}) collective-permute-start(bf16[256,1536]{1,0:T(8,128)(2,1)S(1)} %convolution_convert_fusion), channel_id=1, source_target_pairs={{0,2},{1,3},{2,4},{3,5},{4,6},{5,7},{6,8},{7,9},{8,10},{9,11},{10,... | collective-permute-start | bytes 2359304 | tf_op jit(solution)/shard_map/ppermute | solution.py:16
  254.3 22.5 %collective-permute-start.17 = (bf16[256,1536]{1,0:T(8,128)(2,1)S(1)}, bf16[256,1536]{1,0:T(8,128)(2,1)S(1)}, u32[]{:S(2)}, u32[]{:S(2)}) collective-permute-start(bf16[256,1536]{1,0:T(8,128)(2,1)S(1)} %convolution_convert_fusion), channel_id=1, source_target_pairs={{0,4},{1,5},{2,6},{3,7},{4,8},{5,9},{6,10},{7,11},{8,12},{9,13},{1... | collective-permute-start | bytes 2359304 | tf_op jit(solution)/shard_map/ppermute | solution.py:16
  279.9 38.4 %collective-permute-start.19 = (bf16[512,1536]{1,0:T(8,128)(2,1)}, bf16[512,1536]{1,0:T(8,128)(2,1)}, u32[]{:S(2)}, u32[]{:S(2)}) collective-permute-start(bf16[512,1536]{1,0:T(8,128)(2,1)} %fusion.15), channel_id=1, source_target_pairs={{0,1},{1,0},{2,3},{3,2},{4,5},{5,4},{6,7},{7,6},{8,9},{9,8},{10,11... | collective-permute-start | bytes 4718600 | tf_op jit(solution)/shard_map/ppermute | solution.py:21
  282.4 58.8 %collective-permute-start.22 = (bf16[84,1536]{1,0:T(8,128)(2,1)}, bf16[84,1536]{1,0:T(8,128)(2,1)}, u32[]{:S(2)}, u32[]{:S(2)}) collective-permute-start(bf16[84,1536]{1,0:T(8,128)(2,1)} %get-tuple-element.48), channel_id=1, source_target_pairs={{0,24},{1,25},{2,26},{3,27},{4,28},{5,29},{6,30},{7,31},{8,0},{9,1... | collective-permute-start | bytes 774152 | tf_op jit(solution)/shard_map/ppermute | solution.py:118
  311.6 29.6 %collective-permute-start.21 = (bf16[84,1536]{1,0:T(8,128)(2,1)S(1)}, bf16[84,1536]{1,0:T(8,128)(2,1)}, u32[]{:S(2)}, u32[]{:S(2)}) collective-permute-start(bf16[84,1536]{1,0:T(8,128)(2,1)S(1)} %get-tuple-element.49), channel_id=1, source_target_pairs={{0,16},{1,17},{2,18},{3,19},{4,20},{5,21},{6,22},{7,23},{8,24},{9,... | collective-permute-start | bytes 774152 | tf_op jit(solution)/shard_map/ppermute | solution.py:118
  314.2 27.0 %collective-permute-start.20 = (bf16[84,1536]{1,0:T(8,128)(2,1)S(1)}, bf16[84,1536]{1,0:T(8,128)(2,1)}, u32[]{:S(2)}, u32[]{:S(2)}) collective-permute-start(bf16[84,1536]{1,0:T(8,128)(2,1)S(1)} %get-tuple-element.47), channel_id=1, source_target_pairs={{0,8},{1,9},{2,10},{3,11},{4,12},{5,13},{6,14},{7,15},{8,16},{9,17... | collective-permute-start | bytes 774152 | tf_op jit(solution)/shard_map/ppermute | solution.py:118
  (14 other events, 176.8 us)
Sparse Core Ops, SparseCore 0:
  11.5 99.5 all-gather.1
